TPU v7x, 256 devices: a whole 4x4x8 slice. The times are simulated.
256 devices in a mesh: segment: 8 (over z), expert: 8 (over y, core), dp: 4 (over x).
Axes of the slice: x: 4, y: 4, z: 8, core: 2. Of those that a mesh axis runs over, the one named last changes fastest.
Arguments:
- state_in: bfloat16 [8, 4, 4096, 2048], P('segment', None, ('expert', 'dp')), may hold values from -6 to 6
- entering: bfloat16 [1, 4, 4096, 2048], P(None, None, ('expert', 'dp')), may hold values from -6 to 6
- saved: bfloat16 [8, 2, 2, 4096, 2048], P('segment', None, None, ('expert', 'dp')), may hold values from -6 to 6
- route_ids: int32 [8, 2, 4, 2, 4096, 6], P('segment', None, None, None, ('expert', 'dp')), may hold values from 0 to 63, as said below
- gate_vals: float32 [8, 2, 4, 2, 4096, 6], P('segment', None, None, None, ('expert', 'dp')), may hold values from 0.25 to 1
- w_gate: bfloat16 [8, 8, 2048, 1408], P('segment', 'expert', None, 'dp'), may hold values from -0.125 to 0.125
- w_up: bfloat16 [8, 8, 2048, 1408], P('segment', 'expert', None, 'dp'), may hold values from -0.125 to 0.125
- w_down: bfloat16 [8, 8, 1408, 2048], P('segment', 'expert', 'dp'), may hold values from -0.15625 to 0.15625
- gains: float32 [8, 2, 2048], P('segment'), may hold values from 0.5 to 2
Outputs:
- state_out: bfloat16 [8, 4, 4096, 2048], P('segment', None, ('expert', 'dp'))
Inputs may be any that keep to these rules, and one draw needn't show every extreme that they name: `route_ids`: the ids of one token are distinct, and a token names at most one id under 4. Within each block of 128 consecutive tokens (the tokens of one device) an id under 4 is named by at most 8 tokens. For every section, slot, unit and sublayer some id under 4 is named by exactly 8 tokens in every block, and every block has an id under 4 named by exactly 8 of its tokens.
All inputs are finite; a program needn't handle non-finite values.
Results may differ from a plain program's by a relative error of at most 0.017.
Values may be sent and summed in bfloat16 or wider, within the bound.
No kernel may reach another device: no remote copies, remote signals or barrier semaphores. Data moves between devices by JAX's collectives and lax.ppermute only.
A program may use at most 128 MiB of HBM per device.

v0:
```python
import jax
import jax.numpy as jnp
from jax import lax
from jax.sharding import PartitionSpec as P

CAP = 8
SLOTS = 2


EPSILON = 1e-06
CONTRACT_LAST = (((1,), (1,)), ((), ()))


def from_behind(value, axis, steps):
    count = lax.axis_size(axis)
    first, last = (max(0, -steps), min(count, count - steps))
    return lax.ppermute(value, axis, [(source, source + steps) for source in range(first, last)])


def route_tables(block_ids, block_gates, expert_count):
    expert_range = jnp.arange(expert_count, dtype=jnp.int32)
    matches = block_ids[:, :, None] == expert_range[None, None, :]
    routed = jnp.sum(matches.astype(jnp.int32), axis=1)
    weighting = jnp.sum(
        jnp.where(matches, block_gates[:, :, None], jnp.zeros_like(block_gates[:, :, None])), axis=1
    )
    earlier = jnp.cumsum(routed, axis=0) - routed
    slot_range = jnp.arange(CAP, dtype=jnp.int32)
    chosen = (routed[:, :, None] == 1) & (earlier[:, :, None] == slot_range[None, None, :])
    row_total = block_ids.shape[0]
    slot_total = expert_count * CAP
    flat = chosen.reshape(row_total, slot_total)
    row_range = jnp.arange(row_total, dtype=jnp.int32)
    slot_numbers = jnp.arange(slot_total, dtype=jnp.int32)
    slot_token = jnp.sum(jnp.where(flat, row_range[:, None], 0), axis=0)
    slot_live = jnp.any(flat, axis=0)
    token_slot = jnp.sum(jnp.where(flat, slot_numbers[None, :], 0), axis=1)
    token_live = jnp.any(flat, axis=1)
    slot_gate = jnp.sum(
        jnp.where(chosen, weighting[:, :, None], jnp.zeros_like(weighting[:, :, None])), axis=0
    )
    return (slot_token, slot_live, slot_gate.reshape(slot_total), token_slot, token_live)


def norm_rows(values, norm_gain):
    inverse_rms = lax.rsqrt(jnp.mean(values * values, axis=-1, keepdims=True) + EPSILON)
    return ((values * inverse_rms * norm_gain).astype(jnp.bfloat16), inverse_rms)


def norm_back(values, inverse_rms, norm_gain, delta, grad_normed):
    weighted = norm_gain * grad_normed
    cubed = inverse_rms * inverse_rms * inverse_rms
    return (
        delta
        + inverse_rms * weighted
        - values * cubed * jnp.sum(weighted * values, axis=-1, keepdims=True) / values.shape[-1]
    )


def pick_rows(tables, normed):
    taken = jnp.take(normed, tables[0], axis=0)
    return jnp.where(tables[1][:, None], taken, jnp.zeros_like(taken))


def grad_rows(tables, delta):
    taken = tables[2][:, None] * jnp.take(delta, tables[0], axis=0)
    return jnp.where(tables[1][:, None], taken, jnp.zeros_like(taken)).astype(jnp.bfloat16)


def add_routes(tables, expert_rows):
    taken = jnp.take(tables[2][:, None] * expert_rows, tables[3], axis=0)
    return jnp.where(tables[4][:, None], taken, jnp.zeros_like(taken))


def sum_routes(tables, expert_rows):
    taken = jnp.take(expert_rows, tables[3], axis=0)
    return jnp.where(tables[4][:, None], taken, jnp.zeros_like(taken))


def owner_forward(hidden_rows, layer):
    gate_pre = jnp.dot(hidden_rows, layer[0], preferred_element_type=jnp.float32)
    up_pre = jnp.dot(hidden_rows, layer[1], preferred_element_type=jnp.float32)
    return (gate_pre, up_pre)


def owner_output(gate_pre, up_pre, layer):
    activation = (jax.nn.silu(gate_pre) * up_pre).astype(jnp.bfloat16)
    return jnp.dot(activation, layer[2], preferred_element_type=jnp.float32).astype(jnp.bfloat16)


def owner_back(grad_in_rows, gate_pre, up_pre, layer):
    grad_act = lax.dot_general(
        grad_in_rows, layer[2], CONTRACT_LAST, preferred_element_type=jnp.float32
    )
    sigmoid_gate = jax.nn.sigmoid(gate_pre)
    grad_gate = (grad_act * up_pre * sigmoid_gate * (1.0 + gate_pre * (1.0 - sigmoid_gate))).astype(
        jnp.bfloat16
    )
    grad_up = (grad_act * gate_pre * sigmoid_gate).astype(jnp.bfloat16)
    grad_hidden = lax.dot_general(
        grad_gate, layer[0], CONTRACT_LAST, preferred_element_type=jnp.float32
    )
    grad_hidden = grad_hidden + lax.dot_general(
        grad_up, layer[1], CONTRACT_LAST, preferred_element_type=jnp.float32
    )
    return grad_hidden.astype(jnp.bfloat16)


def send_rows(slot_rows, dest_count, dp_count):
    unit_count = slot_rows.shape[0]
    model_width = slot_rows.shape[2]
    grid = slot_rows.reshape(unit_count, dest_count, 1, CAP, model_width)
    copies = jnp.broadcast_to(grid, (unit_count, dest_count, dp_count, CAP, model_width))
    spread = copies.reshape(unit_count, dest_count * dp_count * CAP, model_width)
    return lax.all_to_all(spread, ("expert", "dp"), split_axis=1, concat_axis=1, tiled=True)


def return_rows(partials, dest_count, dp_count):
    unit_count = partials.shape[0]
    model_width = partials.shape[2]
    backward = lax.all_to_all(partials, ("expert", "dp"), split_axis=1, concat_axis=1, tiled=True)
    grid = backward.reshape(unit_count, dest_count, dp_count, CAP, model_width).astype(jnp.float32)
    return jnp.sum(grid, axis=2).reshape(unit_count, dest_count * CAP, model_width)


def pair_items(lower_items, upper_items):
    return jnp.concatenate([jnp.stack(lower_items), jnp.stack(upper_items)], axis=1)


def local(state_in, entering, saved, route_ids, gate_vals, w_gate, w_up, w_down, gains):
    dest_count = lax.axis_size("expert")
    expert_count = dest_count // 2
    slot_width = expert_count * CAP
    dp_count = lax.axis_size("dp")
    segment_count = lax.axis_size("segment")
    segment_place = lax.axis_index("segment")
    at_bottom = segment_place == 0
    at_top = segment_place == segment_count - 1
    own_layer = (w_gate[0, 0], w_up[0, 0], w_down[0, 0])
    gain_first = gains[0, 0]
    gain_second = gains[0, 1]
    current = state_in[0]
    result = current
    for slot_index in range(SLOTS):
        ids_here = route_ids[0, slot_index]
        gates_here = gate_vals[0, slot_index]
        tables = [
            [
                route_tables(
                    ids_here[unit_index, sub_index], gates_here[unit_index, sub_index], expert_count
                )
                for sub_index in range(2)
            ]
            for unit_index in range(4)
        ]
        start_first = current[0].astype(jnp.float32)
        start_second = current[1].astype(jnp.float32)
        delta_first = current[2].astype(jnp.float32)
        delta_second = current[3].astype(jnp.float32)
        kept_first = saved[0, slot_index, 0].astype(jnp.float32)
        kept_second = saved[0, slot_index, 1].astype(jnp.float32)
        normed_start_first, scale_start_first = norm_rows(start_first, gain_first)
        normed_kept_first, scale_kept_first = norm_rows(kept_first, gain_first)
        normed_start_second, scale_start_second = norm_rows(start_second, gain_second)
        normed_kept_second, scale_kept_second = norm_rows(kept_second, gain_second)
        outgoing = pair_items(
            [
                pick_rows(tables[0][0], normed_start_first),
                pick_rows(tables[2][0], normed_kept_first),
            ],
            [
                pick_rows(tables[1][1], normed_start_second),
                pick_rows(tables[3][1], normed_kept_second),
            ],
        )
        arrived = send_rows(outgoing, dest_count, dp_count)
        row_count = arrived.shape[1]
        model_width = arrived.shape[2]
        gate_pre, up_pre = owner_forward(arrived.reshape(2 * row_count, model_width), own_layer)
        partials = owner_output(gate_pre, up_pre, own_layer).reshape(2, row_count, model_width)
        returned = return_rows(partials, dest_count, dp_count)
        kept_gate = gate_pre[row_count:]
        kept_up = up_pre[row_count:]
        lower = returned[:, :slot_width]
        upper = returned[:, slot_width:]
        middle_start_first = start_first + add_routes(tables[0][0], lower[0])
        middle_kept_first = kept_first + add_routes(tables[2][0], lower[1])
        middle_start_second = start_second + add_routes(tables[1][1], upper[0])
        middle_kept_second = kept_second + add_routes(tables[3][1], upper[1])
        normed_middle_first, scale_middle_first = norm_rows(middle_start_first, gain_second)
        normed_inner_first, scale_inner_first = norm_rows(middle_kept_first, gain_second)
        normed_middle_second, scale_middle_second = norm_rows(middle_start_second, gain_first)
        normed_inner_second, scale_inner_second = norm_rows(middle_kept_second, gain_first)
        outgoing = pair_items(
            [
                pick_rows(tables[1][0], normed_middle_second),
                pick_rows(tables[3][0], normed_inner_second),
                grad_rows(tables[3][0], delta_second),
            ],
            [
                pick_rows(tables[0][1], normed_middle_first),
                pick_rows(tables[2][1], normed_inner_first),
                grad_rows(tables[2][1], delta_first),
            ],
        )
        arrived = send_rows(outgoing, dest_count, dp_count)
        gate_mid, up_mid = owner_forward(
            arrived[0:2].reshape(2 * row_count, model_width), own_layer
        )
        partials = jnp.stack(
            [
                owner_output(gate_mid[:row_count], up_mid[:row_count], own_layer),
                owner_back(arrived[2], gate_mid[row_count:], up_mid[row_count:], own_layer),
            ]
        )
        returned = return_rows(partials, dest_count, dp_count)
        lower = returned[:, :slot_width]
        upper = returned[:, slot_width:]
        forward_second = (middle_start_second + add_routes(tables[1][0], lower[0])).astype(
            jnp.bfloat16
        )
        inner_second = norm_back(
            middle_kept_second,
            scale_inner_second,
            gain_first,
            delta_second,
            sum_routes(tables[3][0], lower[1]),
        )
        forward_first = (middle_start_first + add_routes(tables[0][1], upper[0])).astype(
            jnp.bfloat16
        )
        inner_first = norm_back(
            middle_kept_first,
            scale_inner_first,
            gain_second,
            delta_first,
            sum_routes(tables[2][1], upper[1]),
        )
        outgoing = pair_items(
            [grad_rows(tables[2][0], inner_first)], [grad_rows(tables[3][1], inner_second)]
        )
        arrived = send_rows(outgoing, dest_count, dp_count)
        partials = owner_back(arrived[0], kept_gate, kept_up, own_layer)[None]
        returned = return_rows(partials, dest_count, dp_count)
        backward_first = norm_back(
            kept_first,
            scale_kept_first,
            gain_first,
            inner_first,
            sum_routes(tables[2][0], returned[0, :slot_width]),
        ).astype(jnp.bfloat16)
        backward_second = norm_back(
            kept_second,
            scale_kept_second,
            gain_second,
            inner_second,
            sum_routes(tables[3][1], returned[0, slot_width:]),
        ).astype(jnp.bfloat16)
        result = jnp.stack([forward_first, forward_second, backward_first, backward_second])
        if slot_index + 1 < SLOTS:
            arriving = entering[slot_index]
            upward = from_behind(jnp.stack([forward_first, backward_second]), "segment", 1)
            downward = from_behind(jnp.stack([forward_second, backward_first]), "segment", -1)
            acts_up = upward[0]
            grads_up = upward[1]
            acts_down = downward[0]
            grads_down = downward[1]
            current = jnp.stack(
                [
                    jnp.where(at_bottom, arriving[0], acts_up),
                    jnp.where(at_top, arriving[1], acts_down),
                    jnp.where(at_top, arriving[2], grads_down),
                    jnp.where(at_bottom, arriving[3], grads_up),
                ]
            )
    return result[None]


def solution(mesh):
    in_specs = (
        P("segment", None, ("expert", "dp"), None),
        P(None, None, ("expert", "dp"), None),
        P("segment", None, None, ("expert", "dp"), None),
        P("segment", None, None, None, ("expert", "dp"), None),
        P("segment", None, None, None, ("expert", "dp"), None),
        P("segment", "expert", None, "dp"),
        P("segment", "expert", None, "dp"),
        P("segment", "expert", "dp", None),
        P("segment", None, None),
    )
    out_specs = P("segment", None, ("expert", "dp"), None)
    return jax.shard_map(local, mesh=mesh, in_specs=in_specs, out_specs=out_specs, check_vma=False)
```

profile of v0, /device:TPU:96, one launch (start us, length us, event | category | flops | bytes accessed | tf_op | source)
XLA Modules:
  0.0 886.7 jit_solution(17482659930919373416)
XLA Ops:
  104.0 2.9 fusion.64
  113.7 3.3 broadcast_in_dim.1091
  117.0 7.8 all-to-all-start
  170.0 3.5 copy.202
  173.5 7.9 all-to-all-start.1
  190.2 18.7 %all-to-all-done.1 = bf16[2,256,2048]{2,0,1:T(2,128)(2,1)S(1)} async-done(((bf16[2,256,2048]{2,0,1:T(2,128)(2,1)}), bf16[2,256,2048]{2,0,1:T(2,128)(2,1)S(1)}, u32[]{:S(2)}, u32[]{:S(2)}) %all-to-all-start.1) | async-done | bytes 2097184 | tf_op jit(solution)/shard_map/all_to_all | solution.py:121
  227.6 2.8 gather_fusion.8
  236.4 3.6 multiply_convert_fusion.7
  245.1 4.1 broadcast_in_dim.1131
  249.6 5.2 all-to-all-start.2
  266.6 39.1 %all-to-all-done.2 = bf16[3,256,2048]{2,0,1:T(4,128)(2,1)} async-done(((bf16[3,256,2048]{2,0,1:T(4,128)(2,1)}), bf16[3,256,2048]{2,0,1:T(4,128)(2,1)}, u32[]{:S(2)}, u32[]{:S(2)}) %all-to-all-start.2) | async-done | bytes 3145760 | tf_op jit(solution)/shard_map/all_to_all | solution.py:115
  305.7 4.2 slice.499
  313.6 4.5 slice.502
  321.7 3.9 copy.219
  325.6 5.3 all-to-all-start.3
  346.0 12.3 %all-to-all-done.3 = bf16[2,256,2048]{2,0,1:T(2,128)(2,1)S(1)} async-done(((bf16[2,256,2048]{2,0,1:T(2,128)(2,1)}), bf16[2,256,2048]{2,0,1:T(2,128)(2,1)S(1)}, u32[]{:S(2)}, u32[]{:S(2)}) %all-to-all-start.3) | async-done | bytes 2097184 | tf_op jit(solution)/shard_map/all_to_all | solution.py:121
  366.4 4.5 fusion.78
  372.2 3.0 fusion.88
  375.2 2.8 gather_fusion.17
  379.7 3.6 fusion.80
  388.0 8.0 reduce.68
  396.0 3.0 reshape.1705
  398.9 4.9 all-to-all-start.4
  406.5 14.4 %all-to-all-done.4 = bf16[32,2,8192]{2,1,0:T(2,128)(2,1)S(1)} async-done(((bf16[32,2,8192]{2,1,0:T(2,128)(2,1)}), bf16[32,2,8192]{2,1,0:T(2,128)(2,1)S(1)}, u32[]{:S(2)}, u32[]{:S(2)}) %all-to-all-start.4) | async-done | bytes 1048608 | tf_op jit(solution)/shard_map/all_to_all | solution.py:115
  420.9 3.4 reshape.1706
  429.1 2.9 copy.388
  432.1 9.1 %reduce.69 = bf16[256,2048]{1,0:T(8,128)(2,1)} reduce(bf16[256,1,2048]{2,1,0:T(2,128)(2,1)} %bitcast.525, bf16[]{:T(256)} %broadcast.1161), dimensions={1}, to_apply=%bitcast.513.reduce_sub_computation | reduce | bytes 2097154
  441.2 2.9 reshape.1707
  444.1 5.1 all-to-all-start.5
  454.5 4.1 fusion.115
  458.6 7.5 all-to-all-done.5
  466.2 5.8 reshape.1708
  471.9 3.8 copy.274
  490.5 5.2 collective-permute-start
  508.8 8.9 %collective-permute-done = bf16[2,128,2048]{2,1,0:T(8,128)(2,1)} collective-permute-done((bf16[2,128,2048]{2,1,0:T(8,128)(2,1)}, bf16[2,128,2048]{2,1,0:T(8,128)(2,1)}, u32[]{:S(2)}, u32[]{:S(2)}) %collective-permute-start) | collective-permute-done | bytes 1048608 | tf_op jit(solution)/shard_map/ppermute | solution.py:17
  517.7 6.4 collective-permute-done.1
  537.5 3.3 broadcast_in_dim.1159
  540.9 4.8 all-to-all-start.6
  549.9 23.2 %all-to-all-done.6 = bf16[2,256,2048]{2,0,1:T(2,128)(2,1)} async-done(((bf16[2,256,2048]{2,0,1:T(2,128)(2,1)}), bf16[2,256,2048]{2,0,1:T(2,128)(2,1)}, u32[]{:S(2)}, u32[]{:S(2)}) %all-to-all-start.6) | async-done | bytes 2097184 | tf_op jit(solution)/shard_map/all_to_all | solution.py:115
  579.2 3.5 copy.237
  582.8 5.2 all-to-all-start.7
  604.7 10.6 %all-to-all-done.7 = bf16[2,256,2048]{2,0,1:T(2,128)(2,1)} async-done(((bf16[2,256,2048]{2,0,1:T(2,128)(2,1)}), bf16[2,256,2048]{2,0,1:T(2,128)(2,1)}, u32[]{:S(2)}, u32[]{:S(2)}) %all-to-all-start.7) | async-done | bytes 2097184 | tf_op jit(solution)/shard_map/all_to_all | solution.py:121
  615.3 4.2 convert_reduce_fusion.1
  636.9 4.0 multiply_convert_fusion.2
  650.1 4.5 broadcast_in_dim.1195
  654.6 5.2 all-to-all-start.8
  660.4 50.5 %all-to-all-done.8 = bf16[3,256,2048]{2,0,1:T(4,128)(2,1)} async-done(((bf16[3,256,2048]{2,0,1:T(4,128)(2,1)}), bf16[3,256,2048]{2,0,1:T(4,128)(2,1)}, u32[]{:S(2)}, u32[]{:S(2)}) %all-to-all-start.8) | async-done | bytes 3145760 | tf_op jit(solution)/shard_map/all_to_all | solution.py:115
  710.9 4.2 slice.537
  718.8 4.5 slice.540
  726.8 3.6 copy.254
  730.5 5.3 all-to-all-start.9
  750.9 12.4 %all-to-all-done.9 = bf16[2,256,2048]{2,0,1:T(2,128)(2,1)S(1)} async-done(((bf16[2,256,2048]{2,0,1:T(2,128)(2,1)}), bf16[2,256,2048]{2,0,1:T(2,128)(2,1)S(1)}, u32[]{:S(2)}, u32[]{:S(2)}) %all-to-all-start.9) | async-done | bytes 2097184 | tf_op jit(solution)/shard_map/all_to_all | solution.py:121
  771.3 4.0 multiply_reduce_fusion.1
  781.5 3.5 multiply_subtract_fusion
  789.0 8.0 reduce.70
  797.1 3.0 reshape.1709
  800.0 4.9 all-to-all-start.10
  811.2 10.8 %all-to-all-done.10 = bf16[32,2,8192]{2,1,0:T(2,128)(2,1)S(1)} async-done(((bf16[32,2,8192]{2,1,0:T(2,128)(2,1)}), bf16[32,2,8192]{2,1,0:T(2,128)(2,1)S(1)}, u32[]{:S(2)}, u32[]{:S(2)}) %all-to-all-start.10) | async-done | bytes 1048608 | tf_op jit(solution)/shard_map/all_to_all | solution.py:115
  822.0 3.4 reshape.1710
  831.9 7.8 reduce.71
  839.7 3.3 reshape.1711
  843.0 4.7 all-to-all-start.11
  851.6 13.1 %all-to-all-done.11 = bf16[32,2,8192]{2,1,0:T(2,128)(2,1)} async-done(((bf16[32,2,8192]{2,1,0:T(2,128)(2,1)}), bf16[32,2,8192]{2,1,0:T(2,128)(2,1)}, u32[]{:S(2)}, u32[]{:S(2)}) %all-to-all-start.11) | async-done | bytes 1048608 | tf_op jit(solution)/shard_map/all_to_all | solution.py:121
  864.7 5.8 reshape.1712
  (1104 shorter events, 422.9 us)
Async XLA Ops:
  0.0 168.7 %copy-start = (bf16[1,1,352,2048]{3,2,1,0:T(8,128)(2,1)S(1)}, bf16[1,1,352,2048]{3,2,1,0:T(8,128)(2,1)}, u32[]{:S(2)}) copy-start(bf16[1,1,352,2048]{3,2,1,0:T(8,128)(2,1)} %param.22) | copy-start | bytes 4325380
  8.3 22.6 %copy-start.62 = (s32[128,4]{1,0:T(8,128)}, s32[128,4]{1,0:T(8,128)S(1)}, u32[]{:S(2)}) copy-start(s32[128,4]{1,0:T(8,128)S(1)} %copy.239) | copy-start | bytes 6148
  26.1 37.5 %copy-start.110 = (s32[128,4]{0,1:T(4,128)}, s32[128,4]{0,1:T(4,128)S(1)}, u32[]{:S(2)}) copy-start(s32[128,4]{0,1:T(4,128)S(1)} %copy.215) | copy-start | bytes 6148
  26.4 41.9 %copy-start.112 = (s32[128,4]{0,1:T(4,128)}, s32[128,4]{0,1:T(4,128)S(1)}, u32[]{:S(2)}) copy-start(s32[128,4]{0,1:T(4,128)S(1)} %copy.212) | copy-start | bytes 6148
  27.5 43.9 %copy-start.118 = (s32[128,4]{0,1:T(4,128)}, s32[128,4]{0,1:T(4,128)S(1)}, u32[]{:S(2)}) copy-start(s32[128,4]{0,1:T(4,128)S(1)} %copy.206) | copy-start | bytes 6148
  31.7 59.2 %copy-start.1 = (bf16[1,2,2,128,2048]{4,3,2,1,0:T(8,128)(2,1)S(1)}, bf16[1,2,2,128,2048]{4,3,2,1,0:T(8,128)(2,1)}, u32[]{:S(2)}) copy-start(bf16[1,2,2,128,2048]{4,3,2,1,0:T(8,128)(2,1)} %param.17) | copy-start | bytes 6291460
  34.2 56.7 %copy-start.114 = (s32[128,4]{0,1:T(4,128)}, s32[128,4]{0,1:T(4,128)S(1)}, u32[]{:S(2)}) copy-start(s32[128,4]{0,1:T(4,128)S(1)} %copy.241) | copy-start | bytes 6148
  73.8 17.1 %copy-start.116 = (s32[128,4]{0,1:T(4,128)}, s32[128,4]{0,1:T(4,128)S(1)}, u32[]{:S(2)}) copy-start(s32[128,4]{0,1:T(4,128)S(1)} %copy.244) | copy-start | bytes 6148
  77.8 13.1 %copy-start.107 = (s32[128,4]{0,1:T(4,128)}, s32[128,4]{0,1:T(4,128)S(1)}, u32[]{:S(2)}) copy-start(s32[128,4]{0,1:T(4,128)S(1)} %copy.250) | copy-start | bytes 6148
  117.0 13.7 %copy-start.14 = (bf16[1,4,128,2048]{3,2,1,0:T(8,128)(2,1)S(1)}, bf16[1,4,128,2048]{3,2,1,0:T(8,128)(2,1)}, u32[]{:S(2)}) copy-start(bf16[1,4,128,2048]{3,2,1,0:T(8,128)(2,1)} %param.15) | copy-start | bytes 6291460
  117.0 46.8 %all-to-all-start = ((bf16[2,256,2048]{2,0,1:T(2,128)(2,1)}), bf16[2,256,2048]{2,0,1:T(2,128)(2,1)}, u32[]{:S(2)}, u32[]{:S(2)}) async-start(bf16[2,256,2048]{2,0,1:T(2,128)(2,1)} %bitcast.517), calls=%async_computation | async-start | bytes 4194304 | tf_op jit(solution)/shard_map/all_to_all | solution.py:115
  132.2 25.4 %copy-start.43 = (f32[128,2048]{1,0:T(8,128)S(1)}, f32[128,2048]{1,0:T(8,128)}, u32[]{:S(2)}) copy-start(f32[128,2048]{1,0:T(8,128)} %get-tuple-element.145) | copy-start | bytes 3145732
  136.4 22.6 %copy-start.294 = (s32[32]{0:T(128)}, s32[32]{0:T(128)S(1)}, u32[]{:S(2)}) copy-start(s32[32]{0:T(128)S(1)} %reduce_sum.1063) | copy-start | bytes 388
  138.6 20.4 %copy-start.296 = (s32[32]{0:T(128)}, s32[32]{0:T(128)S(1)}, u32[]{:S(2)}) copy-start(s32[32]{0:T(128)S(1)} %reduce_sum.1051) | copy-start | bytes 388
  141.4 17.6 %copy-start.196 = (s32[1024]{0:T(1024)}, s32[1024]{0:T(1024)S(1)}, u32[]{:S(2)}) copy-start(s32[1024]{0:T(1024)S(1)} %pad_clamp_fusion.20) | copy-start | bytes 12292
  141.4 17.6 %copy-start.197 = (s32[1024]{0:T(1024)}, s32[1024]{0:T(1024)S(1)}, u32[]{:S(2)}) copy-start(s32[1024]{0:T(1024)S(1)} %pad_clamp_fusion.23) | copy-start | bytes 12292
  173.5 35.3 %all-to-all-start.1 = ((bf16[2,256,2048]{2,0,1:T(2,128)(2,1)}), bf16[2,256,2048]{2,0,1:T(2,128)(2,1)S(1)}, u32[]{:S(2)}, u32[]{:S(2)}) async-start(bf16[2,256,2048]{2,0,1:T(2,128)(2,1)} %copy.202), calls=%async_computation.1 | async-start | bytes 4194304 | tf_op jit(solution)/shard_map/all_to_all | solution.py:121
  249.4 9.7 %copy-start.123 = (s32[128,4]{0,1:T(4,128)S(1)}, s32[128,4]{0,1:T(4,128)}, u32[]{:S(2)}) copy-start(s32[128,4]{0,1:T(4,128)} %copy.231) | copy-start | bytes 6148
  249.4 9.7 %copy-start.164 = (pred[128,4]{0,1:T(4,128)(4,1)S(1)}, pred[128,4]{0,1:T(4,128)(4,1)}, u32[]{:S(2)}) copy-start(pred[128,4]{0,1:T(4,128)(4,1)} %broadcast_compare_fusion.5) | copy-start | bytes 1540
  249.4 10.4 %copy-start.122 = (s32[128,4]{0,1:T(4,128)S(1)}, s32[128,4]{0,1:T(4,128)}, u32[]{:S(2)}) copy-start(s32[128,4]{0,1:T(4,128)} %copy.234) | copy-start | bytes 6148
  249.4 10.4 %copy-start.163 = (pred[128,4]{0,1:T(4,128)(4,1)S(1)}, pred[128,4]{0,1:T(4,128)(4,1)}, u32[]{:S(2)}) copy-start(pred[128,4]{0,1:T(4,128)(4,1)} %broadcast_compare_fusion.4) | copy-start | bytes 1540
  249.4 11.1 %copy-start.115 = (s32[128,4]{0,1:T(4,128)S(1)}, s32[128,4]{0,1:T(4,128)}, u32[]{:S(2)}) copy-start(s32[128,4]{0,1:T(4,128)} %copy-done.114) | copy-start | bytes 6148
  249.4 11.1 %copy-start.158 = (pred[128,4]{0,1:T(4,128)(4,1)S(1)}, pred[128,4]{0,1:T(4,128)(4,1)}, u32[]{:S(2)}) copy-start(pred[128,4]{0,1:T(4,128)(4,1)} %broadcast_compare_fusion.3) | copy-start | bytes 1540
  249.4 11.8 %copy-start.117 = (s32[128,4]{0,1:T(4,128)S(1)}, s32[128,4]{0,1:T(4,128)}, u32[]{:S(2)}) copy-start(s32[128,4]{0,1:T(4,128)} %copy-done.116) | copy-start | bytes 6148
  249.4 11.8 %copy-start.157 = (pred[128,4]{0,1:T(4,128)(4,1)S(1)}, pred[128,4]{0,1:T(4,128)(4,1)}, u32[]{:S(2)}) copy-start(pred[128,4]{0,1:T(4,128)(4,1)} %broadcast_compare_fusion.2) | copy-start | bytes 1540
  249.4 12.5 %copy-start.108 = (s32[128,4]{0,1:T(4,128)S(1)}, s32[128,4]{0,1:T(4,128)}, u32[]{:S(2)}) copy-start(s32[128,4]{0,1:T(4,128)} %copy-done.107) | copy-start | bytes 6148
  249.5 12.5 %copy-start.161 = (pred[128,4]{0,1:T(4,128)(4,1)S(1)}, pred[128,4]{0,1:T(4,128)(4,1)}, u32[]{:S(2)}) copy-start(pred[128,4]{0,1:T(4,128)(4,1)} %broadcast_compare_fusion) | copy-start | bytes 1540
  249.5 13.2 %copy-start.105 = (s32[128,4]{0,1:T(4,128)S(1)}, s32[128,4]{0,1:T(4,128)}, u32[]{:S(2)}) copy-start(s32[128,4]{0,1:T(4,128)} %copy-done.104) | copy-start | bytes 6148
  249.5 13.1 %copy-start.159 = (pred[128,4]{0,1:T(4,128)(4,1)S(1)}, pred[128,4]{0,1:T(4,128)(4,1)}, u32[]{:S(2)}) copy-start(pred[128,4]{0,1:T(4,128)(4,1)} %broadcast_compare_fusion.1) | copy-start | bytes 1540
  249.5 13.9 %copy-start.91 = (s32[1,1,128,6]{2,3,1,0:T(8,128)S(1)}, s32[1,1,128,6]{2,3,1,0:T(8,128)}, u32[]{:S(2)}) copy-start(s32[1,1,128,6]{2,3,1,0:T(8,128)} %copy-done.90) | copy-start | bytes 9220
  249.5 13.9 %copy-start.120 = (s32[128,4]{0,1:T(4,128)S(1)}, s32[128,4]{0,1:T(4,128)}, u32[]{:S(2)}) copy-start(s32[128,4]{0,1:T(4,128)} %copy.209) | copy-start | bytes 6148
  249.5 13.9 %copy-start.168 = (pred[128,4]{0,1:T(4,128)(4,1)S(1)}, pred[128,4]{0,1:T(4,128)(4,1)}, u32[]{:S(2)}) copy-start(pred[128,4]{0,1:T(4,128)(4,1)} %broadcast_compare_fusion.10) | copy-start | bytes 1540
  249.5 14.5 %copy-start.89 = (s32[1,1,128,6]{2,3,1,0:T(8,128)S(1)}, s32[1,1,128,6]{2,3,1,0:T(8,128)}, u32[]{:S(2)}) copy-start(s32[1,1,128,6]{2,3,1,0:T(8,128)} %copy-done.88) | copy-start | bytes 9220
  249.5 14.5 %copy-start.119 = (s32[128,4]{0,1:T(4,128)S(1)}, s32[128,4]{0,1:T(4,128)}, u32[]{:S(2)}) copy-start(s32[128,4]{0,1:T(4,128)} %copy-done.118) | copy-start | bytes 6148
  249.5 14.5 %copy-start.167 = (pred[128,4]{0,1:T(4,128)(4,1)S(1)}, pred[128,4]{0,1:T(4,128)(4,1)}, u32[]{:S(2)}) copy-start(pred[128,4]{0,1:T(4,128)(4,1)} %broadcast_compare_fusion.11) | copy-start | bytes 1540
  249.5 15.2 %copy-start.87 = (s32[1,1,128,6]{2,3,1,0:T(8,128)S(1)}, s32[1,1,128,6]{2,3,1,0:T(8,128)}, u32[]{:S(2)}) copy-start(s32[1,1,128,6]{2,3,1,0:T(8,128)} %copy-done.86) | copy-start | bytes 9220
  249.6 15.8 %copy-start.85 = (s32[1,1,128,6]{2,3,1,0:T(8,128)S(1)}, s32[1,1,128,6]{2,3,1,0:T(8,128)}, u32[]{:S(2)}) copy-start(s32[1,1,128,6]{2,3,1,0:T(8,128)} %copy-done.84) | copy-start | bytes 9220
  249.6 56.1 %all-to-all-start.2 = ((bf16[3,256,2048]{2,0,1:T(4,128)(2,1)}), bf16[3,256,2048]{2,0,1:T(4,128)(2,1)}, u32[]{:S(2)}, u32[]{:S(2)}) async-start(bf16[3,256,2048]{2,0,1:T(4,128)(2,1)} %bitcast.515), calls=%async_computation.2 | async-start | bytes 8388608 | tf_op jit(solution)/shard_map/all_to_all | solution.py:115
  255.5 54.4 %copy-start.292 = (s32[32]{0:T(128)}, s32[32]{0:T(128)S(1)}, u32[]{:S(2)}) copy-start(s32[32]{0:T(128)S(1)} %reduce_sum.1102) | copy-start | bytes 388
  255.6 54.3 %copy-start.289 = (s32[32]{0:T(128)}, s32[32]{0:T(128)S(1)}, u32[]{:S(2)}) copy-start(s32[32]{0:T(128)S(1)} %reduce_sum.1090) | copy-start | bytes 388
  255.7 54.2 %copy-start.282 = (s32[32]{0:T(128)}, s32[32]{0:T(128)S(1)}, u32[]{:S(2)}) copy-start(s32[32]{0:T(128)S(1)} %reduce_sum.1133) | copy-start | bytes 388
  255.8 54.1 %copy-start.276 = (s32[32]{0:T(128)}, s32[32]{0:T(128)S(1)}, u32[]{:S(2)}) copy-start(s32[32]{0:T(128)S(1)} %reduce_sum.1121) | copy-start | bytes 388
  325.6 32.8 %all-to-all-start.3 = ((bf16[2,256,2048]{2,0,1:T(2,128)(2,1)}), bf16[2,256,2048]{2,0,1:T(2,128)(2,1)S(1)}, u32[]{:S(2)}, u32[]{:S(2)}) async-start(bf16[2,256,2048]{2,0,1:T(2,128)(2,1)} %copy.219), calls=%async_computation.3 | async-start | bytes 4194304 | tf_op jit(solution)/shard_map/all_to_all | solution.py:121
  396.0 9.9 %copy-start.255 = (s32[128]{0:T(128)S(1)}, s32[128]{0:T(128)}, u32[]{:S(2)}) copy-start(s32[128]{0:T(128)} %get-tuple-element.111) | copy-start | bytes 1540
  398.9 21.9 %all-to-all-start.4 = ((bf16[32,2,8192]{2,1,0:T(2,128)(2,1)}), bf16[32,2,8192]{2,1,0:T(2,128)(2,1)S(1)}, u32[]{:S(2)}, u32[]{:S(2)}) async-start(bf16[32,2,8192]{2,1,0:T(2,128)(2,1)} %reshape.1705), calls=%async_computation.4 | async-start | bytes 2097152 | tf_op jit(solution)/shard_map/all_to_all | solution.py:115
  444.1 22.1 %all-to-all-start.5 = ((bf16[32,2,8192]{2,1,0:T(2,128)(2,1)}), bf16[32,2,8192]{2,1,0:T(2,128)(2,1)}, u32[]{:S(2)}, u32[]{:S(2)}) async-start(bf16[32,2,8192]{2,1,0:T(2,128)(2,1)} %reshape.1707), calls=%async_computation.5 | async-start | bytes 2097152 | tf_op jit(solution)/shard_map/all_to_all | solution.py:121
  489.3 9.9 %copy-start.284 = (pred[4,8]{1,0:T(4,128)(4,1)S(1)}, pred[4,8]{1,0:T(4,128)(4,1)}, u32[]{:S(2)}) copy-start(pred[4,8]{1,0:T(4,128)(4,1)} %get-tuple-element.53) | copy-start | bytes 100
  489.3 10.5 %copy-start.285 = (pred[4,8]{1,0:T(4,128)(4,1)S(1)}, pred[4,8]{1,0:T(4,128)(4,1)}, u32[]{:S(2)}) copy-start(pred[4,8]{1,0:T(4,128)(4,1)} %get-tuple-element.57) | copy-start | bytes 100
  489.3 11.2 %copy-start.286 = (pred[4,8]{1,0:T(4,128)(4,1)S(1)}, pred[4,8]{1,0:T(4,128)(4,1)}, u32[]{:S(2)}) copy-start(pred[4,8]{1,0:T(4,128)(4,1)} %get-tuple-element.45) | copy-start | bytes 100
  489.4 11.8 %copy-start.287 = (pred[4,8]{1,0:T(4,128)(4,1)S(1)}, pred[4,8]{1,0:T(4,128)(4,1)}, u32[]{:S(2)}) copy-start(pred[4,8]{1,0:T(4,128)(4,1)} %get-tuple-element.49) | copy-start | bytes 100
  489.4 12.3 %copy-start.109 = (s32[128,4]{0,1:T(4,128)S(1)}, s32[128,4]{0,1:T(4,128)}, u32[]{:S(2)}) copy-start(s32[128,4]{0,1:T(4,128)} %copy-done.107) | copy-start | bytes 6148
  489.4 12.3 %copy-start.162 = (pred[128,4]{0,1:T(4,128)(4,1)S(1)}, pred[128,4]{0,1:T(4,128)(4,1)}, u32[]{:S(2)}) copy-start(pred[128,4]{0,1:T(4,128)(4,1)} %broadcast_compare_fusion) | copy-start | bytes 1540
  490.5 13.9 %copy-start.45 = (bf16[128,2048]{1,0:T(8,128)(2,1)S(1)}, bf16[128,2048]{1,0:T(8,128)(2,1)}, u32[]{:S(2)}) copy-start(bf16[128,2048]{1,0:T(8,128)(2,1)} %get-tuple-element.126) | copy-start | bytes 1572868
  490.5 27.2 %collective-permute-start = (bf16[2,128,2048]{2,1,0:T(8,128)(2,1)}, bf16[2,128,2048]{2,1,0:T(8,128)(2,1)}, u32[]{:S(2)}, u32[]{:S(2)}) collective-permute-start(bf16[2,128,2048]{2,1,0:T(8,128)(2,1)} %pad_maximum_fusion.2), channel_id=1, source_target_pairs={{0,32},{32,64},{64,96},{96,128},{128,160},{160,192},{192,224},{1,3... | collective-permute-start | bytes 3145736 | tf_op jit(solution)/shard_map/ppermute | solution.py:17
  496.7 27.4 %collective-permute-start.1 = (bf16[2,128,2048]{2,1,0:T(8,128)(2,1)}, bf16[2,128,2048]{2,1,0:T(8,128)(2,1)}, u32[]{:S(2)}, u32[]{:S(2)}) collective-permute-start(bf16[2,128,2048]{2,1,0:T(8,128)(2,1)} %pad_maximum_fusion.3), channel_id=1, source_target_pairs={{32,0},{64,32},{96,64},{128,96},{160,128},{192,160},{224,192},{33,... | collective-permute-start | bytes 3145736 | tf_op jit(solution)/shard_map/ppermute | solution.py:17
  540.9 32.2 %all-to-all-start.6 = ((bf16[2,256,2048]{2,0,1:T(2,128)(2,1)}), bf16[2,256,2048]{2,0,1:T(2,128)(2,1)}, u32[]{:S(2)}, u32[]{:S(2)}) async-start(bf16[2,256,2048]{2,0,1:T(2,128)(2,1)} %bitcast.518), calls=%async_computation.6 | async-start | bytes 4194304 | tf_op jit(solution)/shard_map/all_to_all | solution.py:115
  582.8 10.3 %copy-start.280 = (pred[4,8]{1,0:T(4,128)(4,1)S(1)}, pred[4,8]{1,0:T(4,128)(4,1)}, u32[]{:S(2)}) copy-start(pred[4,8]{1,0:T(4,128)(4,1)} %get-tuple-element.37) | copy-start | bytes 100
  582.8 11.6 %copy-start.278 = (pred[4,8]{1,0:T(4,128)(4,1)S(1)}, pred[4,8]{1,0:T(4,128)(4,1)}, u32[]{:S(2)}) copy-start(pred[4,8]{1,0:T(4,128)(4,1)} %get-tuple-element.41) | copy-start | bytes 100
  582.8 12.8 %copy-start.277 = (s32[32]{0:T(128)S(1)}, s32[32]{0:T(128)}, u32[]{:S(2)}) copy-start(s32[32]{0:T(128)} %copy-done.276) | copy-start | bytes 388
  582.8 32.5 %all-to-all-start.7 = ((bf16[2,256,2048]{2,0,1:T(2,128)(2,1)}), bf16[2,256,2048]{2,0,1:T(2,128)(2,1)}, u32[]{:S(2)}, u32[]{:S(2)}) async-start(bf16[2,256,2048]{2,0,1:T(2,128)(2,1)} %copy.237), calls=%async_computation.7 | async-start | bytes 4194304 | tf_op jit(solution)/shard_map/all_to_all | solution.py:121
  654.6 56.2 %all-to-all-start.8 = ((bf16[3,256,2048]{2,0,1:T(4,128)(2,1)}), bf16[3,256,2048]{2,0,1:T(4,128)(2,1)}, u32[]{:S(2)}, u32[]{:S(2)}) async-start(bf16[3,256,2048]{2,0,1:T(4,128)(2,1)} %bitcast.516), calls=%async_computation.8 | async-start | bytes 8388608 | tf_op jit(solution)/shard_map/all_to_all | solution.py:115
  730.5 32.8 %all-to-all-start.9 = ((bf16[2,256,2048]{2,0,1:T(2,128)(2,1)}), bf16[2,256,2048]{2,0,1:T(2,128)(2,1)S(1)}, u32[]{:S(2)}, u32[]{:S(2)}) async-start(bf16[2,256,2048]{2,0,1:T(2,128)(2,1)} %copy.254), calls=%async_computation.9 | async-start | bytes 4194304 | tf_op jit(solution)/shard_map/all_to_all | solution.py:121
  800.0 21.9 %all-to-all-start.10 = ((bf16[32,2,8192]{2,1,0:T(2,128)(2,1)}), bf16[32,2,8192]{2,1,0:T(2,128)(2,1)S(1)}, u32[]{:S(2)}, u32[]{:S(2)}) async-start(bf16[32,2,8192]{2,1,0:T(2,128)(2,1)} %reshape.1709), calls=%async_computation.10 | async-start | bytes 2097152 | tf_op jit(solution)/shard_map/all_to_all | solution.py:115
  843.0 21.7 %all-to-all-start.11 = ((bf16[32,2,8192]{2,1,0:T(2,128)(2,1)}), bf16[32,2,8192]{2,1,0:T(2,128)(2,1)}, u32[]{:S(2)}, u32[]{:S(2)}) async-start(bf16[32,2,8192]{2,1,0:T(2,128)(2,1)} %reshape.1711), calls=%async_computation.11 | async-start | bytes 2097152 | tf_op jit(solution)/shard_map/all_to_all | solution.py:121
  (253 other events, 1107.2 us)
where the time goes:
time: 900 us; the launch traced here: 887 us
  other arithmetic  290 us (32%)
  local copies, waits for them, and re-layouts  266 us (30%)
  waiting for transfers between devices  228 us (25%)
  starting transfers between devices  73.2 us (8%)
  matrix products  25.5 us (3%)
    all_to_all x6, waiting for transfers between devices, send_rows(): lax.all_to_all(spread, ('expert', 'dp'), split_axis=1, concat_axis=1, til...  138 us
    all_to_all x6, waiting for transfers between devices, return_rows(): lax.all_to_all(partials, ('expert', 'dp'), split_axis=1, concat_axis=1, t...  74.7 us
    unnamed x651, local copies, waits for them, and re-layouts  58.9 us
    all_to_all x6, starting transfers between devices, return_rows(): lax.all_to_all(partials, ('expert', 'dp'), split_axis=1, concat_axis=1, t...  33.4 us
    unnamed x4, other arithmetic  32.9 us
    all_to_all x6, starting transfers between devices, send_rows(): lax.all_to_all(spread, ('expert', 'dp'), split_axis=1, concat_axis=1, til...  32.7 us
    gather x16, local copies, waits for them, and re-layouts, pick_rows(): taken = jnp.take(normed, tables[0], axis=0)  28.4 us
    convert_element_type x9, other arithmetic, norm_rows(): (values * inverse_rms * norm_gain).astype(jnp.bfloat16)  24.3 us
  transfers between devices with their start and end apart: 14, of which 13 were waited for; matrix products, arithmetic and copies ran while one was open for 16% of the time, Pallas kernels for 0%

commit v1 on v0

v1 whole, which is shorter than its diff:
```python
import functools

import jax
import jax.numpy as jnp
from jax import lax
from jax.experimental import pallas as pl
from jax.experimental.pallas import tpu as pltpu
from jax.sharding import PartitionSpec as P

CAP = 8
EPSILON = 1e-06
CHUNK = 256
F32 = jnp.float32
BF16 = jnp.bfloat16
NT = (((1,), (1,)), ((), ()))
VMEM_LIMIT = 48 * 1024 * 1024


def dot(a, b):
    return jnp.dot(a, b, preferred_element_type=F32)


def dot_nt(a, b):
    return lax.dot_general(a, b, NT, preferred_element_type=F32)


def whole(shape):
    zeros = (0,) * len(shape)
    return pl.BlockSpec(tuple(shape), lambda i: zeros, memory_space=pltpu.VMEM)


def item(shape, index):
    place = tuple(index) + (0,) * (len(shape) - len(index))
    block = (None,) * len(index) + tuple(shape[len(index):])
    return pl.BlockSpec(block, lambda i: place, memory_space=pltpu.VMEM)


def call(body, operands, out_shapes, scratch, flops, limit=VMEM_LIMIT):
    arrays = [a for a, _ in operands]
    moved = sum(o.size * o.dtype.itemsize for o in out_shapes)
    moved += sum(min(a.size * a.dtype.itemsize, 2**20) for a in arrays)
    return pl.pallas_call(
        body,
        grid=(1,),
        out_shape=out_shapes,
        in_specs=[s for _, s in operands],
        out_specs=[whole(o.shape) for o in out_shapes],
        scratch_shapes=scratch,
        compiler_params=pltpu.CompilerParams(vmem_limit_bytes=limit),
        cost_estimate=pl.CostEstimate(flops=flops, bytes_accessed=moved, transcendentals=0),
    )(*arrays)


def tables_body(place_ref, ids_ref, gates_ref, pick_ref, spread_ref, gate_ref):
    count = ids_ref.shape[0]
    tokens = ids_ref.shape[2]
    half = tokens // 2
    rows = 8 * CAP
    at_bottom = place_ref[0]
    at_top = place_ref[1]
    row = lax.broadcasted_iota(jnp.int32, (rows, tokens), 0)
    lane = lax.broadcasted_iota(jnp.int32, (rows, tokens), 1)
    dest = row >> 3
    slot = (row & 7).astype(F32)
    expert = dest & 3
    dest_sub = dest >> 2
    stream = (lane >= half).astype(jnp.int32)
    t0 = lax.broadcasted_iota(jnp.int32, (tokens, tokens), 0)
    t1 = lax.broadcasted_iota(jnp.int32, (tokens, tokens), 1)
    before = ((t0 < t1) & ((t0 >= half) == (t1 >= half))).astype(F32).astype(BF16)
    end_rows = jnp.where(dest < 4, at_bottom, at_top).astype(F32)

    def step(index, carry):
        order = index & 1
        ids = ids_ref[index]
        gates = gates_ref[index]
        routed = jnp.zeros((rows, tokens), F32)
        weight = jnp.zeros((rows, tokens), F32)
        for k in range(ids.shape[0]):
            hit = ids[k : k + 1, :] == expert
            routed = routed + hit.astype(F32)
            weight = weight + jnp.where(hit, gates[k : k + 1, :], 0.0)
        earlier = dot(routed.astype(BF16), before)
        good = (routed == 1.0) & (earlier == slot) & (dest_sub == (stream ^ order))
        chosen = good.astype(F32)
        weighted = jnp.where(good, weight, 0.0)
        pick_ref[index] = chosen.astype(BF16)
        turned = jnp.transpose(jnp.concatenate([chosen, weighted], axis=0))
        spread_ref[index] = turned[:, :rows].astype(BF16)
        side = lax.broadcasted_iota(jnp.int32, turned.shape, 1)
        gate_ref[index] = jnp.sum(jnp.where(side >= rows, turned, 0.0), axis=1, keepdims=True)
        return carry

    lax.fori_loop(0, count, step, 0)
    for source, target in ((4, count), (7, count + 1)):
        pick_ref[target] = (pick_ref[source].astype(F32) * end_rows).astype(BF16)


def make_tables(place, ids, gates):
    count, _, tokens = ids.shape
    rows = 8 * CAP
    return call(
        tables_body,
        [
            (place, pl.BlockSpec(memory_space=pltpu.SMEM)),
            (ids, whole(ids.shape)),
            (gates, whole(gates.shape)),
        ],
        [
            jax.ShapeDtypeStruct((count + 2, rows, tokens), BF16),
            jax.ShapeDtypeStruct((count, tokens, rows), BF16),
            jax.ShapeDtypeStruct((count, tokens, 1), F32),
        ],
        [],
        10**8,
    )


def by_half(value, first, second):
    half = value.shape[0] // 2
    return jnp.concatenate([value[:half] * first, value[half:] * second], axis=0)


def columns(index):
    return pl.ds(pl.multiple_of(index * CHUNK, CHUNK), CHUNK)


def block_rows(ref, block, cols):
    rows = ref[:, :, cols].astype(F32)[:, block * CAP : (block + 1) * CAP]
    return rows.reshape(ref.shape[0] * CAP, CHUNK).astype(BF16)


def put_rows(out, blocks, cols, first=0):
    for k in range(out.shape[0]):
        start = (first + k) * CAP
        parts = [b[start : start + CAP] for b in blocks]
        rows = parts[0] if len(parts) == 1 else jnp.concatenate(parts, axis=0)
        out[k, :, cols] = rows.astype(BF16)


def fold(value):
    total = value[:, :128]
    for start in range(128, value.shape[1], 128):
        total = total + value[:, start : start + 128]
    return total


def row_total(partial):
    return jnp.sum(partial, axis=-1, keepdims=True)


def inverse_rms(square_partial, width):
    return lax.rsqrt(row_total(square_partial) / width + EPSILON)


def steps_of(width):
    return width // CHUNK


def start_norm(x_ref):
    width = x_ref.shape[1]

    def step(index, total):
        v = x_ref[:, columns(index)].astype(F32)
        return total + fold(v * v)

    total = lax.fori_loop(0, steps_of(width), step, jnp.zeros((x_ref.shape[0], 128), F32))
    return inverse_rms(total, width)


def add_routes(x_ref, ret_refs, block, spread_ref, gate_ref, mid_ref):
    width = x_ref.shape[1]
    spread = spread_ref[...]
    gate = gate_ref[...]

    def step(index, total):
        cols = columns(index)
        m = x_ref[:, cols].astype(F32) + gate * dot(spread, block_rows(ret_refs, block, cols))
        mid_ref[:, cols] = m
        return total + fold(m * m)

    total = lax.fori_loop(0, steps_of(width), step, jnp.zeros((x_ref.shape[0], 128), F32))
    return inverse_rms(total, width)


def back_sums(load, ret_refs, block, spread_ref, gains, work_ref):
    height, width = work_ref.shape
    spread = spread_ref[...]

    def step(index, totals):
        cols = columns(index)
        grad = dot(spread, block_rows(ret_refs, block, cols))
        w = by_half(grad, gains[0][:, cols], gains[1][:, cols])
        work_ref[:, cols] = w
        v = load(cols)
        return (totals[0] + fold(w * v), totals[1] + fold(v * v))

    zero = jnp.zeros((height, 128), F32)
    along, square = lax.fori_loop(0, steps_of(width), step, (zero, zero))
    inv = inverse_rms(square, width)
    return (row_total(along) * (inv * inv * inv) / width, inv)


def local(state_in, entering, saved, route_ids, gate_vals, w_gate, w_up, w_down, gains):
    width = state_in.shape[-1]
    tokens = state_in.shape[-2]
    pair = 2 * tokens
    hidden = w_down.shape[-2]
    dp_count = lax.axis_size("dp")
    segment_count = lax.axis_size("segment")
    expert_devices = lax.axis_size("expert")
    section = lax.axis_index("segment").astype(jnp.int32)
    at_bottom = (section == 0).astype(jnp.int32)
    at_top = (section == segment_count - 1).astype(jnp.int32)
    place = jnp.stack([at_bottom, at_top])
    block_shape = lambda n: [jax.ShapeDtypeStruct((expert_devices, n * CAP, width), BF16)]
    full = (pair, width)

    cut = hidden // 2
    turned_up = jnp.transpose(w_up[0, 0])
    own_a = jnp.concatenate([jnp.transpose(w_gate[0, 0]), turned_up[:cut]])
    own_b = jnp.concatenate([turned_up[cut:], w_down[0, 0]])
    ahead = [(i, (i + 1) % dp_count) for i in range(dp_count)]
    behind = [((i + 1) % dp_count, i) for i in range(dp_count)]
    left_a = lax.ppermute(own_a, "dp", ahead)
    right_b = lax.ppermute(own_b, "dp", behind)
    left_b = lax.ppermute(own_b, "dp", ahead)
    right_a = lax.ppermute(own_a, "dp", behind)
    far_a = lax.ppermute(left_a, "dp", ahead)
    far_b = lax.ppermute(right_b, "dp", behind)
    weights = [own_a, own_b, left_a, left_b, right_a, right_b, far_a, far_b]

    def exchange(blocks):
        return lax.all_to_all(blocks, "expert", split_axis=0, concat_axis=0, tiled=True)

    upward = [(i, i + 1) for i in range(segment_count - 1)]
    downward = [(i + 1, i) for i in range(segment_count - 1)]

    def paired(values):
        turned = jnp.transpose(values[0], (0, 1, 4, 2, 3))
        stream_a = turned[:, 0::2]
        stream_b = jnp.flip(turned[:, 1::2], axis=3)
        both = jnp.concatenate([stream_a, stream_b], axis=4)
        both = jnp.transpose(both, (0, 1, 3, 2, 4))
        return both.reshape((8,) + both.shape[3:])

    ids = paired(route_ids).astype(F32)
    gates = paired(gate_vals)
    choices = ids.shape[1]
    gain_rows = gains[0].reshape(2, width // 128, 128)
    pack_down = jnp.concatenate(
        [ids[4, :, :tokens], ids[7, :, tokens:], gates[4, :, :tokens], gates[7, :, tokens:], gain_rows[0]]
    )
    pack_up = jnp.concatenate(
        [ids[7, :, :tokens], ids[4, :, tokens:], gates[7, :, :tokens], gates[4, :, tokens:], gain_rows[1]]
    )
    above = lax.ppermute(pack_down, "segment", downward)
    below = lax.ppermute(pack_up, "segment", upward)
    part = lambda v, i: v[i * choices : (i + 1) * choices]
    more_ids = jnp.stack(
        [
            jnp.concatenate([part(above, 0), part(below, 1)], axis=1),
            jnp.concatenate([part(below, 0), part(above, 1)], axis=1),
        ]
    )
    more_gates = jnp.stack(
        [
            jnp.concatenate([part(above, 2), part(below, 3)], axis=1),
            jnp.concatenate([part(below, 2), part(above, 3)], axis=1),
        ]
    )
    gain_above = above[4 * choices :].reshape(1, width)
    gain_below = below[4 * choices :].reshape(1, width)
    all_ids = jnp.concatenate([ids, more_ids]).astype(jnp.int32)
    all_gates = jnp.concatenate([gates, more_gates])
    picks, spreads, gate_columns = make_tables(place, all_ids, all_gates)

    pick = lambda t: (picks, item(picks.shape, (t,)))
    spread = lambda t: (spreads, item(spreads.shape, (t,)))
    gate = lambda t: (gate_columns, item(gate_columns.shape, (t,)))
    gain_lines = gains[0].reshape(2, 1, width)
    gain = lambda j: (gain_lines, item(gain_lines.shape, (j,)))
    plain = lambda a: (a, whole(a.shape))
    each = lambda arrays: [plain(a) for a in arrays]
    states = state_in.reshape(2, pair, width)
    state = lambda p: (states, item(states.shape, (p,)))
    keeps = saved.reshape(2, pair, width)
    kept = lambda t: (keeps, item(keeps.shape, (t,)))
    enters = entering.reshape(2, pair, width)
    enter = lambda p: (enters, item(enters.shape, (p,)))
    place_in = (place, pl.BlockSpec(memory_space=pltpu.SMEM))
    big = pltpu.VMEM(full, F32)
    token_flops = 10**8

    def t1(*refs):
        xs, pick_refs = refs[0:4], refs[4:8]
        delta, pick_d, gate_d, ga, gb = refs[8:13]
        outs = refs[13]
        invs = [start_norm(x) for x in xs]

        def step(index, carry):
            cols = columns(index)
            blocks = []
            for x, inv, pick_x in zip(xs, invs, pick_refs):
                v = by_half(x[:, cols].astype(F32) * inv, ga[:, cols], gb[:, cols]).astype(BF16)
                blocks.append(dot(pick_x[...], v))
            g = (gate_d[...] * delta[:, cols].astype(F32)).astype(BF16)
            blocks.append(dot(pick_d[...], g))
            put_rows(outs, blocks, cols)
            return carry

        lax.fori_loop(0, steps_of(width), step, 0)

    (rows1,) = call(
        t1,
        [state(0), kept(0), kept(1), enter(0), pick(0), pick(2), pick(6), pick(10)]
        + [enter(1), pick(11), gate(7), gain(0), gain(1)],
        block_shape(5),
        [],
        2 * token_flops,
    )
    got1 = exchange(rows1)

    def owner(got, blocks, pre_blocks, forward_blocks, back_block, inner_block, kept_pre, keep_blocks, extra):
        out_blocks = forward_blocks + (back_block is not None)
        operands = [plain(got)]
        if extra is not None:
            operands += [plain(extra)]
        if kept_pre is not None:
            array_g, array_u, position = kept_pre
            spec = pl.BlockSpec(
                (dp_count, 64, hidden), lambda i: (0, position, 0), memory_space=pltpu.VMEM
            )
            operands += [(array_g, spec), (array_u, spec)]
        operands += [(w, pl.BlockSpec(memory_space=pl.ANY)) for w in weights]
        outs = block_shape(out_blocks)
        if keep_blocks:
            shape = jax.ShapeDtypeStruct((dp_count, 64 * len(keep_blocks), hidden), F32)
            outs += [shape, shape]

        def body(*refs):
            refs = list(refs)
            take = lambda n: [refs.pop(0) for _ in range(n)]
            ins = take(1)[0]
            extras = take(1)[0] if extra is not None else None
            pre_g, pre_u = take(2) if kept_pre is not None else (None, None)
            sources = take(2 * dp_count)
            out_refs = take(1)[0]
            keep_g, keep_u = take(2) if keep_blocks else (None, None)
            x, wg, wu, wd, acc, sems = refs

            def copies(q, a, b):
                part = lambda ref, start, size: ref.at[pl.ds(start, size)]
                pairs = [
                    (part(a, 0, hidden), wg.at[q]),
                    (part(a, hidden, cut), wu.at[q, pl.ds(0, cut)]),
                    (part(b, 0, cut), wu.at[q, pl.ds(cut, cut)]),
                    (part(b, cut, hidden), wd.at[q]),
                ]
                return [pltpu.make_async_copy(p, t, sems.at[i, q]) for i, (p, t) in enumerate(pairs)]

            for q in range(dp_count):
                for copy in copies(q, sources[2 * q], sources[2 * q + 1]):
                    copy.start()

            def load(index, carry):
                cols = columns(index)
                for b in range(blocks):
                    rows = block_rows(ins, b, cols)
                    if extras is not None:
                        rows = rows + block_rows(extras, 3 + b, cols)
                    x[b * 64 : (b + 1) * 64, cols] = rows
                acc[:, cols] = jnp.zeros((acc.shape[0], CHUNK), F32)
                return carry

            lax.fori_loop(0, steps_of(width), load, 0)

            def quarter(q, carry):
                for copy in copies(q, sources[0], sources[1]):
                    copy.wait()
                if pre_blocks:
                    rows = x[: pre_blocks * 64]
                    gate_pre = dot_nt(rows, wg[q])
                    up_pre = dot_nt(rows, wu[q])
                    for i, b in enumerate(keep_blocks):
                        keep_g[q, i * 64 : (i + 1) * 64] = gate_pre[b * 64 : (b + 1) * 64]
                        keep_u[q, i * 64 : (i + 1) * 64] = up_pre[b * 64 : (b + 1) * 64]
                if forward_blocks:
                    count = forward_blocks * 64
                    fg = gate_pre[:count]
                    act = (fg * jax.nn.sigmoid(fg) * up_pre[:count]).astype(BF16)
                    acc[:count] += dot(act, wd[q])
                if back_block is not None:
                    base = forward_blocks * 64
                    if kept_pre is not None:
                        bg, bu = pre_g[q], pre_u[q]
                    else:
                        bg = gate_pre[inner_block * 64 : (inner_block + 1) * 64]
                        bu = up_pre[inner_block * 64 : (inner_block + 1) * 64]
                    grad_act = dot_nt(x[back_block * 64 : (back_block + 1) * 64], wd[q])
                    sig = jax.nn.sigmoid(bg)
                    grad_gate = (grad_act * bu * sig * (1.0 + bg * (1.0 - sig))).astype(BF16)
                    grad_up = (grad_act * bg * sig).astype(BF16)
                    acc[base : base + 64] += dot(grad_gate, wg[q]) + dot(grad_up, wu[q])
                return carry

            lax.fori_loop(0, dp_count, quarter, 0)

            def store(index, carry):
                cols = columns(index)
                put_rows(out_refs, [acc[b * 64 : (b + 1) * 64, cols] for b in range(out_blocks)], cols)
                return carry

            lax.fori_loop(0, steps_of(width), store, 0)

        held_shape = pltpu.VMEM((dp_count, hidden, width), BF16)
        result = call(
            body,
            operands,
            outs,
            [
                pltpu.VMEM((blocks * 64, width), BF16),
                held_shape,
                held_shape,
                held_shape,
                pltpu.VMEM((out_blocks * 64, width), F32),
                pltpu.SemaphoreType.DMA((4, dp_count)),
            ],
            2 * 64 * width * hidden * dp_count * (2 * pre_blocks + forward_blocks + 3 * (back_block is not None)),
        )
        return result[0], tuple(result[1:])

    out1, kept_pre = owner(got1, 3, 3, 3, None, None, None, (1, 2), None)
    ret1 = exchange(out1)

    def t2(*refs):
        refs = list(refs)
        take = lambda n: [refs.pop(0) for _ in range(n)]
        rets = take(1)[0]
        xs = take(3)
        spread_refs = take(3)
        gate_refs = take(3)
        pick_refs = take(3)
        delta, gate_d, ga, gb = take(4)
        outs = take(1)[0]
        mids = take(3)
        invs = [
            add_routes(xs[i], rets, i, spread_refs[i], gate_refs[i], mids[i]) for i in range(3)
        ]

        def step(index, carry):
            cols = columns(index)
            blocks = []
            for i in range(3):
                v = by_half(mids[i][:, cols] * invs[i], ga[:, cols], gb[:, cols]).astype(BF16)
                blocks.append(dot(pick_refs[i][...], v))
            g = (gate_d[...] * delta[:, cols].astype(F32)).astype(BF16)
            blocks.append(dot(pick_refs[1][...], g))
            put_rows(outs, blocks, cols)
            return carry

        lax.fori_loop(0, steps_of(width), step, 0)

    (rows2,) = call(
        t2,
        [plain(ret1)]
        + [state(0), kept(0), kept(1), spread(0), spread(2), spread(6), gate(0), gate(2), gate(6)]
        + [pick(1), pick(3), pick(7), state(1), gate(3), gain(1), gain(0)],
        block_shape(4),
        [big, big, big],
        3 * token_flops,
    )
    got2 = exchange(rows2)
    out2, inner_pre = owner(got2, 4, 3, 1, 3, 1, None, (2,), None)
    ret2 = exchange(out2)

    def t3(*refs):
        refs = list(refs)
        take = lambda n: [refs.pop(0) for _ in range(n)]
        rets2 = take(1)[0]
        rets1 = take(1)[0]
        x, spread_x, gate_x, delta, spread_d, pick_n, gate_n, ga, gb = take(9)
        inner = take(1)[0]
        outs = take(1)[0]
        mid, work = take(2)
        add_routes(x, rets1, 1, spread_x, gate_x, mid)
        factor, inv = back_sums(lambda c: mid[:, c], rets2, 1, spread_d, (ga, gb), work)

        def step(index, carry):
            cols = columns(index)
            v = delta[:, cols].astype(F32) + inv * work[:, cols] - mid[:, cols] * factor
            inner[:, cols] = v
            put_rows(outs, [dot(pick_n[...], (gate_n[...] * v).astype(BF16))], cols)
            return carry

        lax.fori_loop(0, steps_of(width), step, 0)

    made3 = call(
        t3,
        [plain(ret2)]
        + [plain(ret1)]
        + [kept(0), spread(2), gate(2), state(1), spread(3), pick(2), gate(2), gain(1), gain(0)],
        [jax.ShapeDtypeStruct(full, F32)] + block_shape(1),
        [big, big],
        2 * token_flops,
    )
    inner0 = made3[0]
    got3 = exchange(made3[1])

    def t3b(*refs):
        refs = list(refs)
        take = lambda n: [refs.pop(0) for _ in range(n)]
        rets2 = take(1)[0]
        rets1 = take(1)[0]
        x, spread_x, gate_x, spread_y, gate_y, pick_n, ga, gb = take(8)
        out_a, out_b, out_rows = take(3)
        mid = take(1)[0]
        add_routes(x, rets1, 0, spread_x, gate_x, mid)

        def finish(index, total):
            cols = columns(index)
            v = mid[:, cols] + gate_y[...] * dot(spread_y[...], block_rows(rets2, 0, cols))
            v = v.astype(BF16)
            out_a[:, cols] = v[:tokens]
            out_b[:, cols] = v[tokens:]
            v = v.astype(F32)
            mid[:, cols] = v
            return total + fold(v * v)

        total = lax.fori_loop(0, steps_of(width), finish, jnp.zeros((pair, 128), F32))
        inv = inverse_rms(total, width)

        def step(index, carry):
            cols = columns(index)
            v = by_half(mid[:, cols] * inv, ga[:, cols], gb[:, cols]).astype(BF16)
            out_rows[:, cols] = dot(pick_n[...], v).astype(BF16)
            return carry

        lax.fori_loop(0, steps_of(width), step, 0)

    half_shape = jax.ShapeDtypeStruct((tokens, width), BF16)
    forward_a, forward_b, next_rows = call(
        t3b,
        [plain(ret2)]
        + [plain(ret1)]
        + [state(0), spread(0), gate(0), spread(1), gate(1), pick(8), plain(gain_above), plain(gain_below)],
        [half_shape, half_shape, jax.ShapeDtypeStruct((64, width), BF16)],
        [big],
        2 * token_flops,
    )
    start_a = lax.ppermute(forward_a, "segment", upward)
    start_b = lax.ppermute(forward_b, "segment", downward)

    out3, _ = owner(got3, 1, 0, 0, 0, None, kept_pre + (0,), (), None)
    ret3 = exchange(out3)
    ret3, start_a, start_b = lax.optimization_barrier((ret3, start_a, start_b))

    def t4(*refs):
        refs = list(refs)
        take = lambda n: [refs.pop(0) for _ in range(n)]
        rets3 = take(1)[0]
        inner, x, spread_x, ga, gb, pick_n, gate_n, rows_f = take(8)
        out_a, out_b, rows_up, rows_down = take(4)
        work = take(1)[0]
        factor, inv = back_sums(lambda c: x[:, c].astype(F32), rets3, 0, spread_x, (ga, gb), work)

        def step(index, carry):
            cols = columns(index)
            v = inner[:, cols] + inv * work[:, cols] - x[:, cols].astype(F32) * factor
            v = v.astype(BF16)
            out_a[:, cols] = v[:tokens]
            out_b[:, cols] = v[tokens:]
            g = (gate_n[...] * v.astype(F32)).astype(BF16)
            blocks = [rows_f[:, cols].astype(F32), dot(pick_n[...], g)]
            put_rows(rows_up, blocks, cols)
            put_rows(rows_down, blocks, cols, rows_up.shape[0])
            return carry

        lax.fori_loop(0, steps_of(width), step, 0)

    next_shape = jax.ShapeDtypeStruct((expert_devices // 2, 2 * CAP, width), BF16)
    back_a, back_b, rows_up, rows_down = call(
        t4,
        [plain(ret3)]
        + [plain(inner0), kept(0), spread(2), gain(0), gain(1), pick(9), gate(9), plain(next_rows)],
        [half_shape, half_shape, next_shape, next_shape],
        [big],
        2 * token_flops,
    )
    from_below = lax.ppermute(rows_up, "segment", upward)
    from_above = lax.ppermute(rows_down, "segment", downward)
    rows4 = jnp.concatenate([from_below, from_above])
    back_a, back_b, rows4 = lax.optimization_barrier((back_a, back_b, rows4))
    got4 = exchange(rows4)
    delta_a = lax.ppermute(back_a, "segment", downward)
    delta_b = lax.ppermute(back_b, "segment", upward)
    out4, _ = owner(got4, 2, 1, 1, 1, None, inner_pre + (0,), (), got1)
    ret4 = exchange(out4)

    def merge(place_ref, start_refs, delta_refs, enter_refs, start, delta):
        bottom = place_ref[0] == 1
        top = place_ref[1] == 1

        def step(index, carry):
            cols = columns(index)
            ef = enter_refs[0][:, cols].astype(F32)
            eg = enter_refs[1][:, cols].astype(F32)
            sa, sb = [r[:, cols].astype(F32) for r in start_refs]
            da, db = [r[:, cols].astype(F32) for r in delta_refs]
            start[:, cols] = jnp.concatenate(
                [jnp.where(bottom, ef[:tokens], sa), jnp.where(top, ef[tokens:], sb)]
            )
            if delta is not None:
                delta[:, cols] = jnp.concatenate(
                    [jnp.where(top, eg[:tokens], da), jnp.where(bottom, eg[tokens:], db)]
                )
            return carry

        lax.fori_loop(0, steps_of(width), step, 0)

    def t5(*refs):
        refs = list(refs)
        take = lambda n: [refs.pop(0) for _ in range(n)]
        place_ref = take(1)[0]
        rets4 = take(1)[0]
        rets1 = take(1)[0]
        starts = take(2)
        deltas = take(2)
        entries = take(2)
        (spread_s, gate_s, pick_s, x, spread_x, gate_x, spread_d, pick_d, gate_d, ga, gb) = take(11)
        middle, inner = take(2)
        outs = take(1)[0]
        mid, work = take(2)
        merge(place_ref, starts, deltas, entries, middle, inner)
        inv_s = add_routes(middle, rets4, 0, spread_s, gate_s, middle)
        add_routes(x, rets1, 2, spread_x, gate_x, mid)
        factor, inv = back_sums(lambda c: mid[:, c], rets4, 1, spread_d, (ga, gb), work)

        def step(index, carry):
            cols = columns(index)
            v = by_half(middle[:, cols] * inv_s, ga[:, cols], gb[:, cols]).astype(BF16)
            d = inner[:, cols] + inv * work[:, cols] - mid[:, cols] * factor
            inner[:, cols] = d
            g = (gate_d[...] * d).astype(BF16)
            put_rows(outs, [dot(pick_s[...], v), dot(pick_d[...], g)], cols)
            return carry

        lax.fori_loop(0, steps_of(width), step, 0)

    made5 = call(
        t5,
        [place_in]
        + [plain(ret4)]
        + [plain(ret1)]
        + each([start_a, start_b, delta_a, delta_b])
        + [enter(0), enter(1)]
        + [spread(4), gate(4), pick(5), kept(1), spread(6), gate(6), spread(7), pick(6), gate(6), gain(1), gain(0)],
        [jax.ShapeDtypeStruct(full, F32), jax.ShapeDtypeStruct(full, F32)] + block_shape(2),
        [big, big],
        4 * token_flops,
    )
    middle1, inner1 = made5[0], made5[1]
    got5 = exchange(made5[2])
    out5, _ = owner(got5, 2, 1, 1, 1, None, kept_pre + (1,), (), None)
    ret5 = exchange(out5)

    def t6(*refs):
        refs = list(refs)
        take = lambda n: [refs.pop(0) for _ in range(n)]
        rets5 = take(1)[0]
        middle, inner, x, spread_s, gate_s, spread_x, ga, gb = take(8)
        out = take(1)[0]
        work = take(1)[0]
        factor, inv = back_sums(lambda c: x[:, c].astype(F32), rets5, 1, spread_x, (ga, gb), work)

        def step(index, carry):
            cols = columns(index)
            f = middle[:, cols] + gate_s[...] * dot(spread_s[...], block_rows(rets5, 0, cols))
            out[:pair, cols] = f.astype(BF16)
            v = inner[:, cols] + inv * work[:, cols] - x[:, cols].astype(F32) * factor
            out[pair:, cols] = v.astype(BF16)
            return carry

        lax.fori_loop(0, steps_of(width), step, 0)

    (result,) = call(
        t6,
        [plain(ret5)]
        + [plain(middle1), plain(inner1), kept(1), spread(5), gate(5), spread(6), gain(0), gain(1)],
        [jax.ShapeDtypeStruct((2 * pair, width), BF16)],
        [big],
        2 * token_flops,
    )
    return result.reshape(state_in.shape)


def solution(mesh):
    in_specs = (
        P("segment", None, ("expert", "dp"), None),
        P(None, None, ("expert", "dp"), None),
        P("segment", None, None, ("expert", "dp"), None),
        P("segment", None, None, None, ("expert", "dp"), None),
        P("segment", None, None, None, ("expert", "dp"), None),
        P("segment", "expert", None, "dp"),
        P("segment", "expert", None, "dp"),
        P("segment", "expert", "dp", None),
        P("segment", None, None),
    )
    out_specs = P("segment", None, ("expert", "dp"), None)
    return jax.shard_map(local, mesh=mesh, in_specs=in_specs, out_specs=out_specs, check_vma=False)
```

time: 900 us -> 412 us (0.46); the launches traced: 887 us -> 410 us
  other arithmetic: 290 us -> 4.23 us
  local copies, waits for them, and re-layouts: 266 us -> 17.2 us
  Pallas kernels: 0 us -> 118 us
  waiting for transfers between devices: 228 us -> 114 us
  blocking collectives: 0 us -> 110 us
  starting transfers between devices: 73.2 us -> 46.8 us
  matrix products: 25.5 us -> 0 us
    all_to_all x12 -> x3, waiting for transfers between devices: 213 us -> 13.5 us  [exchange(): lax.all_to_all(blocks, 'expert', split_axis=0, concat_axis=0, tiled=True)]
    pallas_call x0 -> x13, Pallas kernels: none -> 118 us  [call(): pl.pallas_call(body, grid=(1,), out_shape=out_shapes, in_specs=[s for _,...]
    all_to_all x0 -> x7, blocking collectives: none -> 110 us  [exchange(): lax.all_to_all(blocks, 'expert', split_axis=0, concat_axis=0, tiled=True)]
    ppermute x2 -> x14, waiting for transfers between devices: 15.3 us -> 100 us  [the longest x1 43.1 us: local(): far_a = lax.ppermute(left_a, 'dp', ahead)]
    gather x44 -> x0, local copies, waits for them, and re-layouts: 83.3 us -> none  [the longest x16 28.4 us: pick_rows(): taken = jnp.take(normed, tables[0], axis=0)]
    reduce_sum x68 -> x0, other arithmetic: 60 us -> none  [the longest x9 20.1 us: norm_rows(): jnp.mean(values * values, axis=-1, keepdims=True) + EPSILON]
    all_to_all x12 -> x3, starting transfers between devices: 66.2 us -> 11.2 us  [exchange(): lax.all_to_all(blocks, 'expert', split_axis=0, concat_axis=0, tiled=True)]
    another operation x49 -> x5, other arithmetic: 51.4 us -> 0.1 us  [the longest x1 0.08 us: local(): place = jnp.stack([at_bottom, at_top])]
  transfers between devices with their start and end apart: 14 -> 17, of which waited for: 13 -> 10; matrix products, arithmetic and copies ran while one was open for 16% -> 1% of each run, Pallas kernels for 0% -> 10%
where the time goes in v1:
time: 412 us; the launch traced here: 410 us
  Pallas kernels  118 us (29%)
  waiting for transfers between devices  114 us (28%)
  blocking collectives  110 us (27%)
  starting transfers between devices  46.8 us (11%)
  local copies, waits for them, and re-layouts  17.2 us (4%)
  other arithmetic  4.23 us (1%)
    pallas_call x13, Pallas kernels, call(): pl.pallas_call(body, grid=(1,), out_shape=out_shapes, in_specs=[s for _,...  118 us
    all_to_all x7, blocking collectives, exchange(): lax.all_to_all(blocks, 'expert', split_axis=0, concat_axis=0, tiled=True)  110 us
    ppermute x1, waiting for transfers between devices, local(): far_a = lax.ppermute(left_a, 'dp', ahead)  43.1 us
    ppermute x1, waiting for transfers between devices, local(): left_a = lax.ppermute(own_a, 'dp', ahead)  33.3 us
    unnamed x68, local copies, waits for them, and re-layouts  15 us
    all_to_all x3, waiting for transfers between devices, exchange(): lax.all_to_all(blocks, 'expert', split_axis=0, concat_axis=0, tiled=True)  13.5 us
    all_to_all x3, starting transfers between devices, exchange(): lax.all_to_all(blocks, 'expert', split_axis=0, concat_axis=0, tiled=True)  11.2 us
  transfers between devices with their start and end apart: 17, of which 10 were waited for; matrix products, arithmetic and copies ran while one was open for 1% of the time, Pallas kernels for 10%

profile of v1, /device:TPU:96, one launch (start us, length us, event | category | flops | bytes accessed | tf_op | source)
XLA Modules:
  0.0 410.1 jit_solution(448075229586197822)
XLA Ops:
  0.0 1.6 fusion.1
  1.8 1.6 pad_maximum_fusion.refs_1_.refs_3_.refs_4_
  3.4 1.5 collective-permute-start.2
  4.9 1.6 pad_maximum_fusion.1.refs_2_.refs_4_.refs_5_
  6.5 1.7 collective-permute-start.5
  8.3 1.5 collective-permute-start.4
  9.8 0.5 collective-permute-start.3
  10.8 2.0 collective-permute-start
  13.1 4.6 %collective-permute-done = f32[40,128]{1,0:T(8,128)S(1)} collective-permute-done((f32[40,128]{1,0:T(8,128)S(1)}, f32[40,128]{1,0:T(8,128)S(1)}, u32[]{:S(2)}, u32[]{:S(2)}) %collective-permute-start) | collective-permute-done | bytes 20512 | tf_op jit(solution)/shard_map/ppermute | solution.py:257
  17.7 3.8 collective-permute-start.1
  21.5 33.3 %collective-permute-done.2.refs_3_.refs_5_.refs_6_ = bf16[528,2048]{1,0:T(8,128)(2,1)} collective-permute-done((bf16[528,2048]{1,0:T(8,128)(2,1)}, bf16[528,2048]{1,0:T(8,128)(2,1)}, u32[]{:S(2)}, u32[]{:S(2)}) %collective-permute-start.2) | collective-permute-done | bytes 2162720 | tf_op jit(solution)/shard_map/ppermute | solution.py:225
  55.1 1.7 collective-permute-done.5.refs_6_.refs_8_.refs_9_
  56.8 3.0 collective-permute-start.7
  59.9 4.1 shard_map.91
  64.0 2.1 copy-done.2
  66.0 6.6 %shard_map.92 = bf16[8,40,2048]{2,1,0:T(8,128)(2,1)S(1)} custom-call(bf16[2,256,2048]{2,1,0:T(8,128)(2,1)S(1)} %bitcast.57, bf16[2,256,2048]{2,1,0:T(8,128)(2,1)} %bitcast.60, bf16[2,256,2048]{2,1,0:T(8,128)(2,1)} %bitcast.61, bf16[2,256,2048]{2,1,0:T(8,128)(2,1)} %bitcast.68, ...), custom_call_target="tpu_custom_call" | custom-call | flops 200000000 | bytes 8562688 | tf_op jit(solution)/shard_map/pallas_call | solution.py:42
  72.6 23.2 %all_to_all.50.refs_0_.refs_1_ = bf16[8,40,2048]{2,1,0:T(8,128)(2,1)S(1)} all-to-all(bf16[8,40,2048]{2,1,0:T(8,128)(2,1)S(1)} %shard_map.92), channel_id=1, replica_groups=mesh['segment'=8,'expert'=8,'dp'=4] {'expert'}, dimensions={0} | all-to-all | bytes 2621440 | tf_op jit(solution)/shard_map/all_to_all | solution.py:234
  95.8 7.3 %collective-permute-done.4.refs_5_.refs_7_.refs_8_ = bf16[528,2048]{1,0:T(8,128)(2,1)} collective-permute-done((bf16[528,2048]{1,0:T(8,128)(2,1)}, bf16[528,2048]{1,0:T(8,128)(2,1)}, u32[]{:S(2)}, u32[]{:S(2)}) %collective-permute-start.4) | collective-permute-done | bytes 2162720 | tf_op jit(solution)/shard_map/ppermute | solution.py:228
  103.2 43.1 %collective-permute-done.6.refs_7_.refs_9_.refs_10_ = bf16[528,2048]{1,0:T(8,128)(2,1)S(1)} collective-permute-done((bf16[528,2048]{1,0:T(8,128)(2,1)}, bf16[528,2048]{1,0:T(8,128)(2,1)S(1)}, u32[]{:S(2)}, u32[]{:S(2)}) %collective-permute-start.6) | collective-permute-done | bytes 2162720 | tf_op jit(solution)/shard_map/ppermute | solution.py:229
  146.3 1.6 collective-permute-done.7.refs_8_.refs_10_.refs_11_
  147.9 1.4 copy-done.28
  149.3 9.1 %shard_map.93 = (bf16[8,24,2048]{2,1,0:T(8,128)(2,1)S(1)}, f32[4,128,352]{2,1,0:T(8,128)S(1)}, f32[4,128,352]{2,1,0:T(8,128)S(1)}) custom-call(bf16[8,40,2048]{2,1,0:T(8,128)(2,1)S(1)} %all_to_all.50.refs_0_.refs_1_, bf16[528,2048]{1,0:T(8,128)(2,1)} %pad_maximum_fusion.refs_1_.refs_3_.refs_4_, bf16[528,2048]{1,0:T(8,128)(2,1)} %pad_maximum_fusion.1.refs_2_.refs_4_.refs_5_, ...), custom_call_target="tpu_custom_call" | custom-call | flops 3321888768 | bytes 11665408 | tf_op jit(solution)/shard_map/pallas_call | solution.py:42
  158.5 17.5 %all_to_all.51.refs_0_.refs_1_.refs_2_ = bf16[8,24,2048]{2,1,0:T(8,128)(2,1)S(1)} all-to-all(bf16[8,24,2048]{2,1,0:T(8,128)(2,1)S(1)} %get-tuple-element.34), channel_id=1, replica_groups=mesh['segment'=8,'expert'=8,'dp'=4] {'expert'}, dimensions={0} | all-to-all | bytes 1572864 | tf_op jit(solution)/shard_map/all_to_all | solution.py:234
  176.0 9.2 %shard_map.94 = bf16[8,32,2048]{2,1,0:T(8,128)(2,1)S(1)} custom-call(bf16[8,24,2048]{2,1,0:T(8,128)(2,1)S(1)} %all_to_all.51.refs_0_.refs_1_.refs_2_, bf16[2,256,2048]{2,1,0:T(8,128)(2,1)} %bitcast.53, bf16[2,256,2048]{2,1,0:T(8,128)(2,1)} %bitcast.62, bf16[2,256,2048]{2,1,0:T(8,128)(2,1)} %bitcast.63, ...), custom_call_target="tpu_custom_call" | custom-call | flops 300000000 | bytes 8265728 | tf_op jit(solution)/shard_map/pallas_call | solution.py:42
  185.2 18.5 %all_to_all.52.refs_0_ = bf16[8,32,2048]{2,1,0:T(8,128)(2,1)S(1)} all-to-all(bf16[8,32,2048]{2,1,0:T(8,128)(2,1)S(1)} %shard_map.94), channel_id=1, replica_groups=mesh['segment'=8,'expert'=8,'dp'=4] {'expert'}, dimensions={0} | all-to-all | bytes 2097152 | tf_op jit(solution)/shard_map/all_to_all | solution.py:234
  203.7 14.8 %shard_map.95 = (bf16[8,16,2048]{2,1,0:T(8,128)(2,1)S(1)}, f32[4,64,352]{2,1,0:T(8,128)S(1)}, f32[4,64,352]{2,1,0:T(8,128)S(1)}) custom-call(bf16[8,32,2048]{2,1,0:T(8,128)(2,1)S(1)} %all_to_all.52.refs_0_, bf16[528,2048]{1,0:T(8,128)(2,1)} %pad_maximum_fusion.refs_1_.refs_3_.refs_4_, bf16[528,2048]{1,0:T(8,128)(2,1)} %pad_maximum_fusion.1.refs_2_.refs_4_.refs_5_, ...), custom_call_target="tpu_custom_call" | custom-call | flops 3690987520 | bytes 10682368 | tf_op jit(solution)/shard_map/pallas_call | solution.py:42
  218.5 12.8 %all_to_all.53.refs_0_ = bf16[8,16,2048]{2,1,0:T(8,128)(2,1)S(1)} all-to-all(bf16[8,16,2048]{2,1,0:T(8,128)(2,1)S(1)} %get-tuple-element.36), channel_id=1, replica_groups=mesh['segment'=8,'expert'=8,'dp'=4] {'expert'}, dimensions={0} | all-to-all | bytes 1048576 | tf_op jit(solution)/shard_map/all_to_all | solution.py:234
  231.3 6.7 %shard_map.96 = (f32[256,2048]{1,0:T(8,128)S(1)}, bf16[8,8,2048]{2,1,0:T(8,128)(2,1)S(1)}) custom-call(bf16[8,16,2048]{2,1,0:T(8,128)(2,1)S(1)} %all_to_all.53.refs_0_, bf16[8,24,2048]{2,1,0:T(8,128)(2,1)S(1)} %all_to_all.51.refs_0_.refs_1_.refs_2_, bf16[2,256,2048]{2,1,0:T(8,128)(2,1)} %bitcast.64, ...), custom_call_target="tpu_custom_call" | custom-call | flops 200000000 | bytes 6868992 | tf_op jit(solution)/shard_map/pallas_call | solution.py:42
  238.0 1.3 copy-done.13
  239.4 0.7 copy-done.22
  240.0 3.6 all-to-all-start.4
  243.7 1.0 copy-done.6
  244.7 6.6 %shard_map.98 = (bf16[128,2048]{1,0:T(8,128)(2,1)}, bf16[128,2048]{1,0:T(8,128)(2,1)}, bf16[64,2048]{1,0:T(8,128)(2,1)S(1)}) custom-call(bf16[8,16,2048]{2,1,0:T(8,128)(2,1)S(1)} %copy-done.6, bf16[8,24,2048]{2,1,0:T(8,128)(2,1)S(1)} %all_to_all.51.refs_0_.refs_1_.refs_2_, bf16[2,256,2048]{2,1,0:T(8,128)(2,1)} %bitcast.56, ...), custom_call_target="tpu_custom_call" | custom-call | flops 200000000 | bytes 4755456 | tf_op jit(solution)/shard_map/pallas_call | solution.py:42
  251.3 0.7 copy-done.20
  252.0 5.0 %collective-permute-start.8 = (bf16[128,2048]{1,0:T(8,128)(2,1)}, bf16[128,2048]{1,0:T(8,128)(2,1)}, u32[]{:S(2)}, u32[]{:S(2)}) collective-permute-start(bf16[128,2048]{1,0:T(8,128)(2,1)} %get-tuple-element.40), channel_id=1, source_target_pairs={{0,32},{32,64},{64,96},{96,128},{128,160},{160,192},{192,224},{1,3... | collective-permute-start | bytes 1572872 | tf_op jit(solution)/shard_map/ppermute | solution.py:551
  257.0 1.9 collective-permute-start.9
  259.0 1.1 copy-done.8
  260.1 1.1 copy-done.11
  261.3 7.9 %shard_map.97 = bf16[8,8,2048]{2,1,0:T(8,128)(2,1)S(1)} custom-call(bf16[8,8,2048]{2,1,0:T(8,128)(2,1)S(1)} %all-to-all-done.4.refs_0_, f32[4,128,352]{2,1,0:T(8,128)S(1)} %copy-done.8, f32[4,128,352]{2,1,0:T(8,128)S(1)} %copy-done.11, bf16[528,2048]{1,0:T(8,128)(2,1)} %pad_maximum_fusion.refs_1_.refs_3_.refs_4_, ...), custom_call_target="tpu_custom_call" | custom-call | flops 1107296256 | bytes 10354688 | tf_op jit(solution)/shard_map/pallas_call | solution.py:42
  269.1 11.9 %all_to_all.54.refs_0_ = bf16[8,8,2048]{2,1,0:T(8,128)(2,1)S(1)} all-to-all(bf16[8,8,2048]{2,1,0:T(8,128)(2,1)S(1)} %shard_map.97), channel_id=1, replica_groups=mesh['segment'=8,'expert'=8,'dp'=4] {'expert'}, dimensions={0} | all-to-all | bytes 524288 | tf_op jit(solution)/shard_map/all_to_all | solution.py:234
  281.0 5.4 %shard_map.99 = (bf16[128,2048]{1,0:T(8,128)(2,1)S(1)}, bf16[128,2048]{1,0:T(8,128)(2,1)S(1)}, bf16[4,16,2048]{2,1,0:T(8,128)(2,1)S(1)}, bf16[4,16,2048]{2,1,0:T(8,128)(2,1)S(1)}) custom-call(bf16[8,8,2048]{2,1,0:T(8,128)(2,1)S(1)} %all_to_all.54.refs_0_, f32[256,2048]{1,0:T(8,128)} %copy-done.13, bf16[2,256,2048]{2,1,0:T(8,128)(2,1)} %bitcast.65, ...), custom_call_target="tpu_custom_call" | custom-call | flops 200000000 | bytes 4958208 | tf_op jit(solution)/shard_map/pallas_call | solution.py:42
  286.4 0.9 copy-done.25
  287.3 0.8 copy-done.26
  288.1 5.3 %collective-permute-start.10 = (bf16[4,16,2048]{2,1,0:T(8,128)(2,1)S(1)}, bf16[4,16,2048]{2,1,0:T(8,128)(2,1)S(1)}, u32[]{:S(2)}, u32[]{:S(2)}) collective-permute-start(bf16[4,16,2048]{2,1,0:T(8,128)(2,1)S(1)} %get-tuple-element.47), channel_id=1, source_target_pairs={{0,32},{32,64},{64,96},{96,128},{128,160},{160,192},{192,224},{1,3... | collective-permute-start | bytes 786440 | tf_op jit(solution)/shard_map/ppermute | solution.py:590
  293.4 1.9 collective-permute-start.11
  295.3 3.2 collective-permute-done.10
  298.5 5.3 %collective-permute-done.11 = bf16[4,16,2048]{2,1,0:T(8,128)(2,1)S(1)} collective-permute-done((bf16[4,16,2048]{2,1,0:T(8,128)(2,1)S(1)}, bf16[4,16,2048]{2,1,0:T(8,128)(2,1)S(1)}, u32[]{:S(2)}, u32[]{:S(2)}) %collective-permute-start.11) | collective-permute-done | bytes 262176 | tf_op jit(solution)/shard_map/ppermute | solution.py:591
  303.9 0.8 pad_maximum_fusion.2
  304.7 4.1 %all-to-all-start.6 = ((bf16[8,16,2048]{2,1,0:T(8,128)(2,1)}), bf16[8,16,2048]{2,1,0:T(8,128)(2,1)}, u32[]{:S(2)}, u32[]{:S(2)}) async-start(bf16[8,16,2048]{2,1,0:T(8,128)(2,1)} %pad_maximum_fusion.2), calls=%async_computation.6 | async-start | bytes 1048576 | tf_op jit(solution)/shard_map/all_to_all | solution.py:234
  308.9 1.9 collective-permute-start.12
  310.8 5.1 %collective-permute-start.13 = (bf16[128,2048]{1,0:T(8,128)(2,1)}, bf16[128,2048]{1,0:T(8,128)(2,1)}, u32[]{:S(2)}, u32[]{:S(2)}) collective-permute-start(bf16[128,2048]{1,0:T(8,128)(2,1)} %copy-done.25), channel_id=1, source_target_pairs={{0,32},{32,64},{64,96},{96,128},{128,160},{160,192},{192,224},{1,3... | collective-permute-start | bytes 1572872 | tf_op jit(solution)/shard_map/ppermute | solution.py:596
  316.0 3.3 all-to-all-done.6.refs_0_
  319.2 1.0 copy-done.19
  320.2 14.9 %shard_map.100 = bf16[8,16,2048]{2,1,0:T(8,128)(2,1)S(1)} custom-call(bf16[8,16,2048]{2,1,0:T(8,128)(2,1)} %all-to-all-done.6.refs_0_, bf16[8,40,2048]{2,1,0:T(8,128)(2,1)S(1)} %copy-done.4, f32[4,64,352]{2,1,0:T(8,128)S(1)} %copy-done.17, f32[4,64,352]{2,1,0:T(8,128)S(1)} %copy-done.19, bf16[528,2048]{1,0:T(8,128)(2,1)} %pad_maximum_fusion.refs_1_.refs_3_.refs_4_, ...), custom_call_target="tpu_custom_call" | custom-call | flops 2214592512 | bytes 11206656 | tf_op jit(solution)/shard_map/pallas_call | solution.py:42
  335.2 0.8 copy-done.14
  335.9 3.5 all-to-all-start.7
  339.5 10.2 %all-to-all-done.7.refs_1_ = bf16[8,16,2048]{2,1,0:T(8,128)(2,1)S(1)} async-done(((bf16[8,16,2048]{2,1,0:T(8,128)(2,1)}), bf16[8,16,2048]{2,1,0:T(8,128)(2,1)S(1)}, u32[]{:S(2)}, u32[]{:S(2)}) %all-to-all-start.7) | async-done | bytes 524320 | tf_op jit(solution)/shard_map/all_to_all | solution.py:234
  349.7 0.7 copy-done.24
  350.4 11.8 %shard_map.101 = (f32[256,2048]{1,0:T(8,128)}, f32[256,2048]{1,0:T(8,128)}, bf16[8,16,2048]{2,1,0:T(8,128)(2,1)S(1)}) custom-call(s32[2]{0:T(128)S(1)} %copy-done.24, bf16[8,16,2048]{2,1,0:T(8,128)(2,1)S(1)} %all-to-all-done.7.refs_1_, bf16[8,24,2048]{2,1,0:T(8,128)(2,1)S(1)} %all_to_all.51.refs_0_.refs_1_.refs_2_, ...), custom_call_target="tpu_custom_call" | custom-call | flops 400000000 | bytes 13105160 | tf_op jit(solution)/shard_map/pallas_call | solution.py:42
  362.2 12.8 %all_to_all.55.refs_0_ = bf16[8,16,2048]{2,1,0:T(8,128)(2,1)S(1)} all-to-all(bf16[8,16,2048]{2,1,0:T(8,128)(2,1)S(1)} %get-tuple-element.56), channel_id=1, replica_groups=mesh['segment'=8,'expert'=8,'dp'=4] {'expert'}, dimensions={0} | all-to-all | bytes 1048576 | tf_op jit(solution)/shard_map/all_to_all | solution.py:234
  375.0 1.1 copy-done.12
  376.1 14.0 %shard_map.102 = bf16[8,16,2048]{2,1,0:T(8,128)(2,1)S(1)} custom-call(bf16[8,16,2048]{2,1,0:T(8,128)(2,1)S(1)} %all_to_all.55.refs_0_, f32[4,128,352]{2,1,0:T(8,128)S(1)} %copy-done.9, f32[4,128,352]{2,1,0:T(8,128)S(1)} %copy-done.12, bf16[528,2048]{1,0:T(8,128)(2,1)} %pad_maximum_fusion.refs_1_.refs_3_.refs_4_, ...), custom_call_target="tpu_custom_call" | custom-call | flops 2214592512 | bytes 10878976 | tf_op jit(solution)/shard_map/pallas_call | solution.py:42
  390.2 12.8 %all_to_all.56.refs_0_ = bf16[8,16,2048]{2,1,0:T(8,128)(2,1)S(1)} all-to-all(bf16[8,16,2048]{2,1,0:T(8,128)(2,1)S(1)} %shard_map.102), channel_id=1, replica_groups=mesh['segment'=8,'expert'=8,'dp'=4] {'expert'}, dimensions={0} | all-to-all | bytes 1048576 | tf_op jit(solution)/shard_map/all_to_all | solution.py:234
  403.0 7.1 %shard_map.103 = bf16[512,2048]{1,0:T(8,128)(2,1)} custom-call(bf16[8,16,2048]{2,1,0:T(8,128)(2,1)S(1)} %all_to_all.56.refs_0_, f32[256,2048]{1,0:T(8,128)S(1)} %copy-done.15, f32[256,2048]{1,0:T(8,128)} %get-tuple-element.58.refs_2_, bf16[2,256,2048]{2,1,0:T(8,128)(2,1)} %bitcast.67, ...), custom_call_target="tpu_custom_call" | custom-call | flops 200000000 | bytes 6465536 | tf_op jit(solution)/shard_map/pallas_call | solution.py:42
  (86 shorter events, 1.4 us)
Async XLA Ops:
  0.0 1.8 copy-start.29
  1.8 3.1 copy-start.30
  3.4 51.4 %collective-permute-start.2 = (bf16[528,2048]{1,0:T(8,128)(2,1)}, bf16[528,2048]{1,0:T(8,128)(2,1)}, u32[]{:S(2)}, u32[]{:S(2)}) collective-permute-start(bf16[528,2048]{1,0:T(8,128)(2,1)} %pad_maximum_fusion.refs_1_.refs_3_.refs_4_), channel_id=1, source_target_pairs={{0,1},{1,2},{2,3},{3,0},{4,5},{5,6},{6,7},{7,4},{8,9},{9,10},{10,1... | collective-permute-start | bytes 6488072 | tf_op jit(solution)/shard_map/ppermute | solution.py:225
  4.9 5.4 %copy-start.32 = (s32[1,2,4,2,128,6]{4,3,5,2,1,0:T(2,128)S(1)}, s32[1,2,4,2,128,6]{4,3,5,2,1,0:T(2,128)}, u32[]{:S(2)}) copy-start(s32[1,2,4,2,128,6]{4,3,5,2,1,0:T(2,128)} %param.12) | copy-start | bytes 147460
  4.9 5.5 %copy-start.33 = (f32[1,2,4,2,128,6]{4,3,5,2,1,0:T(2,128)S(1)}, f32[1,2,4,2,128,6]{4,3,5,2,1,0:T(2,128)}, u32[]{:S(2)}) copy-start(f32[1,2,4,2,128,6]{4,3,5,2,1,0:T(2,128)} %param.13) | copy-start | bytes 147460
  4.9 5.7 %copy-start.31 = (f32[1,2,2048]{2,1,0:T(2,128)S(1)}, f32[1,2,2048]{2,1,0:T(2,128)}, u32[]{:S(2)}) copy-start(f32[1,2,2048]{2,1,0:T(2,128)} %param.17) | copy-start | bytes 49156
  6.5 50.3 %collective-permute-start.5 = (bf16[528,2048]{1,0:T(8,128)(2,1)}, bf16[528,2048]{1,0:T(8,128)(2,1)}, u32[]{:S(2)}, u32[]{:S(2)}) collective-permute-start(bf16[528,2048]{1,0:T(8,128)(2,1)} %pad_maximum_fusion.1.refs_2_.refs_4_.refs_5_), channel_id=1, source_target_pairs={{1,0},{2,1},{3,2},{0,3},{5,4},{6,5},{7,6},{4,7},{9,8},{10,9},{11,1... | collective-permute-start | bytes 6488072 | tf_op jit(solution)/shard_map/ppermute | solution.py:226
  8.3 94.9 %collective-permute-start.4 = (bf16[528,2048]{1,0:T(8,128)(2,1)}, bf16[528,2048]{1,0:T(8,128)(2,1)}, u32[]{:S(2)}, u32[]{:S(2)}) collective-permute-start(bf16[528,2048]{1,0:T(8,128)(2,1)} %pad_maximum_fusion.refs_1_.refs_3_.refs_4_), channel_id=1, source_target_pairs={{1,0},{2,1},{3,2},{0,3},{5,4},{6,5},{7,6},{4,7},{9,8},{10,9},{11,1... | collective-permute-start | bytes 6488072 | tf_op jit(solution)/shard_map/ppermute | solution.py:228
  9.8 93.3 %collective-permute-start.3 = (bf16[528,2048]{1,0:T(8,128)(2,1)}, bf16[528,2048]{1,0:T(8,128)(2,1)}, u32[]{:S(2)}, u32[]{:S(2)}) collective-permute-start(bf16[528,2048]{1,0:T(8,128)(2,1)} %pad_maximum_fusion.1.refs_2_.refs_4_.refs_5_), channel_id=1, source_target_pairs={{0,1},{1,2},{2,3},{3,0},{4,5},{5,6},{6,7},{7,4},{8,9},{9,10},{10,1... | collective-permute-start | bytes 6488072 | tf_op jit(solution)/shard_map/ppermute | solution.py:227
  10.8 6.9 %collective-permute-start = (f32[40,128]{1,0:T(8,128)S(1)}, f32[40,128]{1,0:T(8,128)S(1)}, u32[]{:S(2)}, u32[]{:S(2)}) collective-permute-start(f32[40,128]{1,0:T(8,128)S(1)} %concatenate.41), channel_id=1, source_target_pairs={{32,0},{64,32},{96,64},{128,96},{160,128},{192,160},{224,192},{33,... | collective-permute-start | bytes 61448 | tf_op jit(solution)/shard_map/ppermute | solution.py:257
  12.9 59.7 %copy-start.23 = (s32[2]{0:T(128)}, s32[2]{0:T(128)S(1)}, u32[]{:S(2)}) copy-start(s32[2]{0:T(128)S(1)} %add_convert_fusion.1.place_ref.refs_0_) | copy-start | bytes 28
  17.7 42.1 %collective-permute-start.1 = (f32[40,128]{1,0:T(8,128)S(1)}, f32[40,128]{1,0:T(8,128)S(1)}, u32[]{:S(2)}, u32[]{:S(2)}) collective-permute-start(f32[40,128]{1,0:T(8,128)S(1)} %concatenate.42), channel_id=1, source_target_pairs={{0,32},{32,64},{64,96},{96,128},{128,160},{160,192},{192,224},{1,3... | collective-permute-start | bytes 61448 | tf_op jit(solution)/shard_map/ppermute | solution.py:258
  54.9 91.4 %collective-permute-start.6 = (bf16[528,2048]{1,0:T(8,128)(2,1)}, bf16[528,2048]{1,0:T(8,128)(2,1)S(1)}, u32[]{:S(2)}, u32[]{:S(2)}) collective-permute-start(bf16[528,2048]{1,0:T(8,128)(2,1)} %collective-permute-done.2.refs_3_.refs_5_.refs_6_), channel_id=1, source_target_pairs={{0,1},{1,2},{2,3},{3,0},{4,5},{5,6},{6,7},{7,4},{8,9},{9,10},{10,1... | collective-permute-start | bytes 6488072 | tf_op jit(solution)/shard_map/ppermute | solution.py:229
  56.8 91.1 %collective-permute-start.7 = (bf16[528,2048]{1,0:T(8,128)(2,1)}, bf16[528,2048]{1,0:T(8,128)(2,1)S(1)}, u32[]{:S(2)}, u32[]{:S(2)}) collective-permute-start(bf16[528,2048]{1,0:T(8,128)(2,1)} %collective-permute-done.5.refs_6_.refs_8_.refs_9_), channel_id=1, source_target_pairs={{1,0},{2,1},{3,2},{0,3},{5,4},{6,5},{7,6},{4,7},{9,8},{10,9},{11,1... | collective-permute-start | bytes 6488072 | tf_op jit(solution)/shard_map/ppermute | solution.py:230
  63.9 217.1 %copy-start = (f32[10,256,1]{2,1,0:T(8,128)}, f32[10,256,1]{2,1,0:T(8,128)S(1)}, u32[]{:S(2)}) copy-start(f32[10,256,1]{2,1,0:T(8,128)S(1)} %get-tuple-element.33.refs_10_.refs_7_.refs_8_.refs_9_.refs_14_.refs_4_.refs_6_.refs_17_.refs_5_) | copy-start | bytes 30724
  63.9 2.1 copy-start.2
  95.8 62.6 %copy-start.3 = (bf16[8,40,2048]{2,1,0:T(8,128)(2,1)}, bf16[8,40,2048]{2,1,0:T(8,128)(2,1)S(1)}, u32[]{:S(2)}) copy-start(bf16[8,40,2048]{2,1,0:T(8,128)(2,1)S(1)} %all_to_all.50.refs_0_.refs_1_) | copy-start | bytes 3932164
  146.3 1.6 copy-start.27
  147.9 1.4 copy-start.28
  158.4 26.7 %copy-start.7 = (f32[4,128,352]{2,1,0:T(8,128)}, f32[4,128,352]{2,1,0:T(8,128)S(1)}, u32[]{:S(2)}) copy-start(f32[4,128,352]{2,1,0:T(8,128)S(1)} %get-tuple-element.38.refs_1_) | copy-start | bytes 2162692
  158.5 26.7 %copy-start.10 = (f32[4,128,352]{2,1,0:T(8,128)}, f32[4,128,352]{2,1,0:T(8,128)S(1)}, u32[]{:S(2)}) copy-start(f32[4,128,352]{2,1,0:T(8,128)S(1)} %get-tuple-element.39.refs_2_) | copy-start | bytes 2162692
  218.5 19.5 %copy-start.16 = (f32[4,64,352]{2,1,0:T(8,128)}, f32[4,64,352]{2,1,0:T(8,128)S(1)}, u32[]{:S(2)}) copy-start(f32[4,64,352]{2,1,0:T(8,128)S(1)} %get-tuple-element.50.refs_2_) | copy-start | bytes 1081348
  218.5 19.5 %copy-start.18 = (f32[4,64,352]{2,1,0:T(8,128)}, f32[4,64,352]{2,1,0:T(8,128)S(1)}, u32[]{:S(2)}) copy-start(f32[4,64,352]{2,1,0:T(8,128)S(1)} %get-tuple-element.51.refs_3_) | copy-start | bytes 1081348
  231.3 6.7 %copy-start.5 = (bf16[8,16,2048]{2,1,0:T(8,128)(2,1)}, bf16[8,16,2048]{2,1,0:T(8,128)(2,1)S(1)}, u32[]{:S(2)}) copy-start(bf16[8,16,2048]{2,1,0:T(8,128)(2,1)S(1)} %all_to_all.53.refs_0_) | copy-start | bytes 1572868
  238.0 1.3 copy-start.13
  239.4 0.7 copy-start.22
  240.0 18.9 %all-to-all-start.4 = ((bf16[8,8,2048]{2,1,0:T(8,128)(2,1)}), bf16[8,8,2048]{2,1,0:T(8,128)(2,1)S(1)}, u32[]{:S(2)}, u32[]{:S(2)}) async-start(bf16[8,8,2048]{2,1,0:T(8,128)(2,1)} %copy-done.22), calls=%async_computation.4 | async-start | bytes 524288 | tf_op jit(solution)/shard_map/all_to_all | solution.py:234
  243.7 1.0 copy-start.6
  251.3 0.7 copy-start.20
  252.0 29.0 %collective-permute-start.8 = (bf16[128,2048]{1,0:T(8,128)(2,1)}, bf16[128,2048]{1,0:T(8,128)(2,1)}, u32[]{:S(2)}, u32[]{:S(2)}) collective-permute-start(bf16[128,2048]{1,0:T(8,128)(2,1)} %get-tuple-element.40), channel_id=1, source_target_pairs={{0,32},{32,64},{64,96},{96,128},{128,160},{160,192},{192,224},{1,3... | collective-permute-start | bytes 1572872 | tf_op jit(solution)/shard_map/ppermute | solution.py:551
  257.0 24.0 %collective-permute-start.9 = (bf16[128,2048]{1,0:T(8,128)(2,1)}, bf16[128,2048]{1,0:T(8,128)(2,1)}, u32[]{:S(2)}, u32[]{:S(2)}) collective-permute-start(bf16[128,2048]{1,0:T(8,128)(2,1)} %get-tuple-element.41), channel_id=1, source_target_pairs={{32,0},{64,32},{96,64},{128,96},{160,128},{192,160},{224,192},{33,... | collective-permute-start | bytes 1572872 | tf_op jit(solution)/shard_map/ppermute | solution.py:552
  259.0 1.1 copy-start.8
  260.1 1.1 copy-start.11
  261.2 19.8 %copy-start.21 = (bf16[64,2048]{1,0:T(8,128)(2,1)S(1)}, bf16[64,2048]{1,0:T(8,128)(2,1)}, u32[]{:S(2)}) copy-start(bf16[64,2048]{1,0:T(8,128)(2,1)} %copy-done.20) | copy-start | bytes 786436
  286.4 0.9 copy-start.25
  287.3 0.8 copy-start.26
  288.1 31.1 %copy-start.4 = (bf16[8,40,2048]{2,1,0:T(8,128)(2,1)S(1)}, bf16[8,40,2048]{2,1,0:T(8,128)(2,1)}, u32[]{:S(2)}) copy-start(bf16[8,40,2048]{2,1,0:T(8,128)(2,1)} %copy-done.3) | copy-start | bytes 3932164
  288.1 31.1 %copy-start.17 = (f32[4,64,352]{2,1,0:T(8,128)S(1)}, f32[4,64,352]{2,1,0:T(8,128)}, u32[]{:S(2)}) copy-start(f32[4,64,352]{2,1,0:T(8,128)} %copy-done.16) | copy-start | bytes 1081348
  288.1 10.4 %collective-permute-start.10 = (bf16[4,16,2048]{2,1,0:T(8,128)(2,1)S(1)}, bf16[4,16,2048]{2,1,0:T(8,128)(2,1)S(1)}, u32[]{:S(2)}, u32[]{:S(2)}) collective-permute-start(bf16[4,16,2048]{2,1,0:T(8,128)(2,1)S(1)} %get-tuple-element.47), channel_id=1, source_target_pairs={{0,32},{32,64},{64,96},{96,128},{128,160},{160,192},{192,224},{1,3... | collective-permute-start | bytes 786440 | tf_op jit(solution)/shard_map/ppermute | solution.py:590
  293.4 10.5 %collective-permute-start.11 = (bf16[4,16,2048]{2,1,0:T(8,128)(2,1)S(1)}, bf16[4,16,2048]{2,1,0:T(8,128)(2,1)S(1)}, u32[]{:S(2)}, u32[]{:S(2)}) collective-permute-start(bf16[4,16,2048]{2,1,0:T(8,128)(2,1)S(1)} %get-tuple-element.48), channel_id=1, source_target_pairs={{32,0},{64,32},{96,64},{128,96},{160,128},{192,160},{224,192},{33,... | collective-permute-start | bytes 786440 | tf_op jit(solution)/shard_map/ppermute | solution.py:591
  304.7 14.5 %all-to-all-start.6 = ((bf16[8,16,2048]{2,1,0:T(8,128)(2,1)}), bf16[8,16,2048]{2,1,0:T(8,128)(2,1)}, u32[]{:S(2)}, u32[]{:S(2)}) async-start(bf16[8,16,2048]{2,1,0:T(8,128)(2,1)} %pad_maximum_fusion.2), calls=%async_computation.6 | async-start | bytes 1048576 | tf_op jit(solution)/shard_map/all_to_all | solution.py:234
  308.9 30.6 %collective-permute-start.12 = (bf16[128,2048]{1,0:T(8,128)(2,1)}, bf16[128,2048]{1,0:T(8,128)(2,1)}, u32[]{:S(2)}, u32[]{:S(2)}) collective-permute-start(bf16[128,2048]{1,0:T(8,128)(2,1)} %copy-done.26), channel_id=1, source_target_pairs={{32,0},{64,32},{96,64},{128,96},{160,128},{192,160},{224,192},{33,... | collective-permute-start | bytes 1572872 | tf_op jit(solution)/shard_map/ppermute | solution.py:595
  310.8 28.7 %collective-permute-start.13 = (bf16[128,2048]{1,0:T(8,128)(2,1)}, bf16[128,2048]{1,0:T(8,128)(2,1)}, u32[]{:S(2)}, u32[]{:S(2)}) collective-permute-start(bf16[128,2048]{1,0:T(8,128)(2,1)} %copy-done.25), channel_id=1, source_target_pairs={{0,32},{32,64},{64,96},{96,128},{128,160},{160,192},{192,224},{1,3... | collective-permute-start | bytes 1572872 | tf_op jit(solution)/shard_map/ppermute | solution.py:596
  319.2 1.0 copy-start.19
  335.1 0.8 copy-start.14
  335.9 13.8 %all-to-all-start.7 = ((bf16[8,16,2048]{2,1,0:T(8,128)(2,1)}), bf16[8,16,2048]{2,1,0:T(8,128)(2,1)S(1)}, u32[]{:S(2)}, u32[]{:S(2)}) async-start(bf16[8,16,2048]{2,1,0:T(8,128)(2,1)} %copy-done.14), calls=%async_computation.7 | async-start | bytes 1048576 | tf_op jit(solution)/shard_map/all_to_all | solution.py:234
  339.4 35.5 %copy-start.9 = (f32[4,128,352]{2,1,0:T(8,128)S(1)}, f32[4,128,352]{2,1,0:T(8,128)}, u32[]{:S(2)}) copy-start(f32[4,128,352]{2,1,0:T(8,128)} %copy-done.7) | copy-start | bytes 2162692
  349.7 0.7 copy-start.24
  375.0 1.1 copy-start.12
  376.1 26.8 %copy-start.1 = (f32[10,256,1]{2,1,0:T(8,128)S(1)}, f32[10,256,1]{2,1,0:T(8,128)}, u32[]{:S(2)}) copy-start(f32[10,256,1]{2,1,0:T(8,128)} %copy-done) | copy-start | bytes 30724
  376.1 26.8 %copy-start.15 = (f32[256,2048]{1,0:T(8,128)S(1)}, f32[256,2048]{1,0:T(8,128)}, u32[]{:S(2)}) copy-start(f32[256,2048]{1,0:T(8,128)} %get-tuple-element.57.refs_1_) | copy-start | bytes 6291460
